TPU v7x, 256 devices: a whole 4x4x8 slice. The times are simulated.
256 devices in a mesh: gz: 16 (over y_lo, z), gx: 4 (over y_hi, core), gy: 4 (over x).
Axes of the slice: x: 4, y: 4 (y_hi: 2, y_lo: 2; y = y_hi * 2 + y_lo), z: 8, core: 2. Of those that a mesh axis runs over, the one named last changes fastest.
Arguments:
- sections: bfloat16 [16, 2560, 2560], P('gz', 'gy', 'gx'), may hold values from -440 to 440
- peaks: int32 [16, 2, 40, 40], P('gz', None, 'gy', 'gx'), may hold values from 0 to 127
- valid: int32 [16, 40, 40], P('gz', 'gy', 'gx'), may hold values 0 or 1
Outputs:
- fit: float32 [16, 6, 40, 40], P('gz', None, 'gy', 'gx')
All inputs are finite; a program needn't handle non-finite values. Where the computation divides by a largest or mean magnitude, that divisor is 1e-20 or more. No bound on the sum of `valid` on one device may be relied on, other than what follows from the above.
Results may differ from a plain program's by a relative error of at most 0.0089.
Values may be sent and summed in bfloat16 or wider, within the bound.
A program may use at most 64 MiB of HBM per device.

v0:
```python
import math

import jax
import jax.numpy as jnp
from jax import lax
from jax.sharding import PartitionSpec as P

PATCH = 128
STRIDE = 64
WIN = 5


def passed_along(value, axis, steps):
    count = lax.axis_size(axis)
    initial, last = (max(0, -steps), min(count, count - steps))
    return lax.ppermute(value, axis, [(source, source + steps) for source in range(initial, last)])


def dft_tables(length):
    index = jnp.arange(length, dtype=jnp.int32)
    phase = (index[:, None] * index[None, :] % length).astype(jnp.float32) * (
        2.0 * math.pi / length
    )
    return (jnp.cos(phase).astype(jnp.bfloat16), jnp.sin(phase).astype(jnp.bfloat16))


def fit_basis(width):
    offsets = (jnp.arange(width, dtype=jnp.int32) - width // 2).astype(jnp.float32)
    ones = jnp.ones((width,), jnp.float32)
    square = offsets * offsets - jnp.mean(offsets * offsets)
    funcs = jnp.stack(
        [
            ones[:, None] * ones[None, :],
            offsets[:, None] * ones[None, :],
            ones[:, None] * offsets[None, :],
            square[:, None] * ones[None, :],
            ones[:, None] * square[None, :],
            offsets[:, None] * offsets[None, :],
        ],
        0,
    )
    return funcs / jnp.sqrt(jnp.sum(funcs * funcs, axis=(1, 2), keepdims=True))


def correlate_row(block, peak_row, valid_row):
    count = block.shape[0]
    length = block.shape[1]
    half = length // 2
    tiles = block.shape[2] // half - 1
    cosine, sine = dft_tables(length)
    columns = block.reshape(count, length, tiles + 1, half)
    patches = jnp.concatenate([columns[:, :, :-1], columns[:, :, 1:]], axis=3)
    energy = jnp.mean(jnp.square(patches.astype(jnp.float32)), axis=(1, 3))
    first_table = jnp.concatenate([cosine, -sine], 0)
    segment_one = jnp.einsum(
        "cnjm,km->cnjk", patches, first_table, preferred_element_type=jnp.float32
    ).astype(jnp.bfloat16)
    second_table = jnp.stack(
        [jnp.stack([cosine, sine], 1), jnp.stack([-sine, cosine], 1)], 0
    ).reshape(2 * length, 2, length)
    spectrum = jnp.einsum(
        "qrn,cnjrk->cqjk",
        second_table,
        segment_one.reshape(count, length, tiles, 2, length),
        preferred_element_type=jnp.float32,
    ).astype(jnp.bfloat16)
    real = spectrum[:, :length].astype(jnp.float32)
    imaginary = spectrum[:, length:].astype(jnp.float32)
    cross_real = real[:-1] * real[1:] + imaginary[:-1] * imaginary[1:]
    cross_imag = real[:-1] * imaginary[1:] - imaginary[:-1] * real[1:]
    cross = jnp.stack([cross_real, cross_imag], 1).astype(jnp.bfloat16)
    third_table = jnp.stack(
        [jnp.stack([cosine, -sine], 1), jnp.stack([sine, cosine], 1)], 0
    ).reshape(2 * length, 2, length)
    inverse_one = jnp.einsum(
        "qrn,crnjk->cqjk", third_table, cross, preferred_element_type=jnp.float32
    ).astype(jnp.bfloat16)
    fourth_table = jnp.stack([cosine, -sine], 0)
    surface = jnp.einsum(
        "crajk,rdk->cajd",
        inverse_one.reshape(count - 1, 2, length, tiles, length),
        fourth_table,
        preferred_element_type=jnp.float32,
    )
    scale = float(length) ** 3 * jnp.sqrt((energy[:-1] + 1e-05) * (energy[1:] + 1e-05))
    corr = surface / scale[:, None, :, None]
    height = jnp.max(jnp.abs(corr), axis=(1, 3)) + 1e-05
    offsets = jnp.arange(WIN, dtype=jnp.int32) - WIN // 2
    positions = jnp.arange(length, dtype=jnp.int32)
    row_pick = (peak_row[:, 0, :, None] + offsets) % length
    col_pick = (peak_row[:, 1, :, None] + offsets) % length
    row_hot = (row_pick[..., None] == positions).astype(jnp.float32)
    col_hot = (col_pick[..., None] == positions).astype(jnp.float32)
    partial_rows = jnp.einsum("cjup,cpjq->cjuq", row_hot, corr, precision=lax.Precision.HIGHEST)
    window = jnp.einsum("cjuq,cjvq->cjuv", partial_rows, col_hot, precision=lax.Precision.HIGHEST)
    coefficient = jnp.einsum(
        "euv,cjuv->cej", fit_basis(WIN), window, precision=lax.Precision.HIGHEST
    )
    return coefficient / height[:, None, :] * valid_row[:, None, :].astype(jnp.float32)


def extend_tile(stacked):
    lower = passed_along(stacked[:, :STRIDE, :], "gy", -1)
    taller = jnp.concatenate([stacked, lower], 1)
    beside = passed_along(taller[:, :, :STRIDE], "gx", -1)
    return jnp.concatenate([taller, beside], 2)


def body(sections, peaks, valid):
    extended = extend_tile(sections)
    following = passed_along(extended, "gz", -1)
    stacked = jnp.concatenate([extended, following], 0)
    patch_rows = sections.shape[1] // STRIDE

    def one_row(index):
        block = lax.dynamic_slice_in_dim(stacked, index * STRIDE, PATCH, axis=1)
        peak_row = lax.dynamic_index_in_dim(peaks, index, 2, False)
        valid_row = lax.dynamic_index_in_dim(valid, index, 1, False)
        return correlate_row(block, peak_row, valid_row)

    result = lax.map(one_row, jnp.arange(patch_rows, dtype=jnp.int32))
    return jnp.transpose(result, (1, 2, 0, 3))


def solution(mesh):
    in_specs = (P("gz", "gy", "gx"), P("gz", None, "gy", "gx"), P("gz", "gy", "gx"))
    out_specs = P("gz", None, "gy", "gx")
    return jax.shard_map(body, mesh=mesh, in_specs=in_specs, out_specs=out_specs, check_vma=False)
```

profile of v0, /device:TPU:9, one launch (start us, length us, event | category | flops | bytes accessed | tf_op | source)
XLA Modules:
  0.0 195.9 jit_solution(13758156889801356262)
XLA Ops:
  0.0 1.8 copy.19
  1.9 1.3 collective-permute-start
  3.2 5.7 %collective-permute-done = bf16[1,64,640]{1,2,0:T(8,128)(2,1)S(1)} collective-permute-done((bf16[1,64,640]{1,2,0:T(8,128)(2,1)S(1)}, bf16[1,64,640]{1,2,0:T(8,128)(2,1)S(1)}, u32[]{:S(2)}, u32[]{:S(2)}) %collective-permute-start) | collective-permute-done | bytes 81952 | tf_op jit(solution)/shard_map/ppermute | solution.py:16
  8.8 3.5 %collective-permute-start.1 = (bf16[1,704,64]{1,2,0:T(8,128)(2,1)S(1)}, bf16[1,704,64]{1,2,0:T(8,128)(2,1)S(1)}, u32[]{:S(2)}, u32[]{:S(2)}) collective-permute-start(bf16[1,704,64]{1,2,0:T(8,128)(2,1)S(1)} %pad_maximum_fusion.10), channel_id=1, source_target_pairs={{4,0},{8,4},{12,8},{5,1},{9,5},{13,9},{6,2},{10,6},{14,10},{7,3},{... | collective-permute-start | bytes 270344 | tf_op jit(solution)/shard_map/ppermute | solution.py:16
  12.3 4.2 %collective-permute-done.1 = bf16[1,704,64]{1,2,0:T(8,128)(2,1)S(1)} collective-permute-done((bf16[1,704,64]{1,2,0:T(8,128)(2,1)S(1)}, bf16[1,704,64]{1,2,0:T(8,128)(2,1)S(1)}, u32[]{:S(2)}, u32[]{:S(2)}) %collective-permute-start.1) | collective-permute-done | bytes 90144 | tf_op jit(solution)/shard_map/ppermute | solution.py:16
  16.6 8.3 %collective-permute-start.2 = (bf16[1,704,704]{1,2,0:T(8,128)(2,1)S(1)}, bf16[1,704,704]{1,2,0:T(8,128)(2,1)S(1)}, u32[]{:S(2)}, u32[]{:S(2)}) collective-permute-start(bf16[1,704,704]{1,2,0:T(8,128)(2,1)S(1)} %pad_maximum_fusion.9), channel_id=1, source_target_pairs={{16,0},{32,16},{48,32},{64,48},{80,64},{96,80},{112,96},{128,112},... | collective-permute-start | bytes 2973704 | tf_op jit(solution)/shard_map/ppermute | solution.py:16
  24.9 20.3 %collective-permute-done.2 = bf16[1,704,704]{1,2,0:T(8,128)(2,1)S(1)} collective-permute-done((bf16[1,704,704]{1,2,0:T(8,128)(2,1)S(1)}, bf16[1,704,704]{1,2,0:T(8,128)(2,1)S(1)}, u32[]{:S(2)}, u32[]{:S(2)}) %collective-permute-start.2) | collective-permute-done | bytes 991264 | tf_op jit(solution)/shard_map/ppermute | solution.py:16
  45.2 1.6 pad_maximum_fusion.8
  46.7 148.5 %while.12 = (s32[]{:T(128)}, f32[10,1,6,10]{3,1,0,2:T(1,128)S(1)}, s32[10]{0:T(128)S(1)}, s32[1,2,10,10]{3,1,2,0:T(2,128)}, bf16[2,704,704]{1,2,0:T(8,128)(2,1)}...) while((s32[]{:T(128)}, f32[10,1,6,10]{3,1,0,2:T(1,128)S(1)}, ...), condition=%wide.region_5.6_spmd, body=%wide.region_0.5_spmd.sunk | while | flops 774986624 | bytes 24838636 | solution.py:121
  47.9 1.3 constant_dynamic-slice_fusion.3
  52.3 0.8 copy.48
  57.6 0.7 dynamic-slice_bitcast_fusion.2
  60.7 0.7 fusion.102
  62.7 1.3 constant_dynamic-slice_fusion.3
  67.2 0.8 copy.48
  72.5 0.7 dynamic-slice_bitcast_fusion.2
  75.5 0.7 fusion.102
  77.6 1.3 constant_dynamic-slice_fusion.3
  82.1 0.8 copy.48
  87.3 0.7 dynamic-slice_bitcast_fusion.2
  90.4 0.7 fusion.102
  92.4 1.3 constant_dynamic-slice_fusion.3
  96.9 0.8 copy.48
  102.2 0.7 dynamic-slice_bitcast_fusion.2
  105.2 0.7 fusion.102
  107.3 1.3 constant_dynamic-slice_fusion.3
  111.8 0.8 copy.48
  117.0 0.7 dynamic-slice_bitcast_fusion.2
  120.1 0.7 fusion.102
  122.2 1.3 constant_dynamic-slice_fusion.3
  126.6 0.8 copy.48
  131.9 0.7 dynamic-slice_bitcast_fusion.2
  134.9 0.7 fusion.102
  137.0 1.3 constant_dynamic-slice_fusion.3
  141.5 0.8 copy.48
  146.7 0.7 dynamic-slice_bitcast_fusion.2
  149.8 0.7 fusion.102
  151.9 1.3 constant_dynamic-slice_fusion.3
  156.3 0.8 copy.48
  161.6 0.7 dynamic-slice_bitcast_fusion.2
  164.6 0.7 fusion.102
  166.7 1.3 constant_dynamic-slice_fusion.3
  171.2 0.8 copy.48
  176.5 0.7 dynamic-slice_bitcast_fusion.2
  181.6 1.3 constant_dynamic-slice_fusion.3
  186.0 0.8 copy.48
  191.3 0.7 dynamic-slice_bitcast_fusion.2
  194.3 0.7 fusion.102
  (448 shorter events, 85.6 us)
Async XLA Ops:
  1.9 7.0 %collective-permute-start = (bf16[1,64,640]{1,2,0:T(8,128)(2,1)S(1)}, bf16[1,64,640]{1,2,0:T(8,128)(2,1)S(1)}, u32[]{:S(2)}, u32[]{:S(2)}) collective-permute-start(bf16[1,64,640]{1,2,0:T(8,128)(2,1)S(1)} %slice.92), channel_id=1, source_target_pairs={{1,0},{2,1},{3,2},{5,4},{6,5},{7,6},{9,8},{10,9},{11,10},{13,12},{... | collective-permute-start | bytes 245768 | tf_op jit(solution)/shard_map/ppermute | solution.py:16
  8.8 7.6 %collective-permute-start.1 = (bf16[1,704,64]{1,2,0:T(8,128)(2,1)S(1)}, bf16[1,704,64]{1,2,0:T(8,128)(2,1)S(1)}, u32[]{:S(2)}, u32[]{:S(2)}) collective-permute-start(bf16[1,704,64]{1,2,0:T(8,128)(2,1)S(1)} %pad_maximum_fusion.10), channel_id=1, source_target_pairs={{4,0},{8,4},{12,8},{5,1},{9,5},{13,9},{6,2},{10,6},{14,10},{7,3},{... | collective-permute-start | bytes 270344 | tf_op jit(solution)/shard_map/ppermute | solution.py:16
  16.6 28.6 %collective-permute-start.2 = (bf16[1,704,704]{1,2,0:T(8,128)(2,1)S(1)}, bf16[1,704,704]{1,2,0:T(8,128)(2,1)S(1)}, u32[]{:S(2)}, u32[]{:S(2)}) collective-permute-start(bf16[1,704,704]{1,2,0:T(8,128)(2,1)S(1)} %pad_maximum_fusion.9), channel_id=1, source_target_pairs={{16,0},{32,16},{48,32},{64,48},{80,64},{96,80},{112,96},{128,112},... | collective-permute-start | bytes 2973704 | tf_op jit(solution)/shard_map/ppermute | solution.py:16
  195.3 0.6 copy-start
where the time goes:
time: 197 us; the launch traced here: 196 us
  local copies, waits for them, and re-layouts  49.7 us (25%)
  other arithmetic  44.9 us (23%)
  waiting for transfers between devices  30.2 us (15%)
  loops' own time  30.1 us (15%)
  matrix products  27.9 us (14%)
  starting transfers between devices  13 us (7%)
    ppermute x3, waiting for transfers between devices, passed_along(): lax.ppermute(value, axis, [(source, source + steps) for source in range(i...  30.2 us
    another operation x1, loops' own time, body(): result = lax.map(one_row, jnp.arange(patch_rows, dtype=jnp.int32))  30.1 us
    ppermute x3, starting transfers between devices, passed_along(): lax.ppermute(value, axis, [(source, source + steps) for source in range(i...  13 us
    dynamic_slice x10, local copies, waits for them, and re-layouts, one_row(): block = lax.dynamic_slice_in_dim(stacked, index * STRIDE, PATCH, axis=1)  12.8 us
    neg x30, other arithmetic, correlate_row(): first_table = jnp.concatenate([cosine, -sine], 0)  8.02 us
    reshape x10, local copies, waits for them, and re-layouts, correlate_row(): segment_one.reshape(count, length, tiles, 2, length)  7.85 us
    squeeze x10, local copies, waits for them, and re-layouts, one_row(): peak_row = lax.dynamic_index_in_dim(peaks, index, 2, False)  6.84 us
    while x20, local copies, waits for them, and re-layouts  6.73 us
  transfers between devices with their start and end apart: 3, of which 3 were waited for; matrix products, arithmetic and copies ran while one was open for 0% of the time, Pallas kernels for 0%

commit v1 on v0

v1 whole, which is shorter than its diff:
```python
import functools
import math

import jax
import jax.numpy as jnp
import ml_dtypes
import numpy as np
from jax import lax
from jax.experimental import pallas as pl
from jax.experimental.pallas import tpu as pltpu
from jax.sharding import PartitionSpec as P

PATCH = 128
STRIDE = 64
WIN = 5
HALF = 64
ROWS = 704
LANES = 768
BLOCKS = 5
PAIRS = 3
F32 = jnp.float32
BF16 = jnp.bfloat16


def host_tables():
    index = np.arange(PATCH)
    phase = ((index[:, None] * index[None, :]) % PATCH).astype(np.float32) * np.float32(
        2.0 * math.pi / PATCH
    )
    rounded = lambda v: v.astype(ml_dtypes.bfloat16).astype(np.float32)
    cosine, sine = rounded(np.cos(phase)), rounded(np.sin(phase))
    first = np.zeros((256, 256), np.float32)
    last = np.zeros((256, 256), np.float32)
    weight = np.where(np.arange(HALF) == 0, 1.0, 2.0).astype(np.float32)
    for w in range(2):
        rows = slice(64 * w, 64 * w + 128)
        real, imag = slice(64 * w, 64 * w + 64), slice(128 + 64 * w, 192 + 64 * w)
        lags = slice(128 * w, 128 * w + 128)
        first[rows, real] = cosine[:HALF].T
        first[rows, imag] = -sine[:HALF].T
        first[rows, 128 + 64 * w] = 0.0
        last[real, lags] = (cosine[:, :HALF] * weight).T
        last[imag, lags] = (-sine[:, :HALF] * weight).T
        last[128 + 64 * w, lags] = cosine[:, HALF]
    nyquist = np.zeros((LANES, 128), np.float32)
    for b in range(BLOCKS):
        for w in range(2):
            start = 128 * b + 64 * w
            nyquist[start : start + 128, b + 64 * w] = cosine[HALF]
    forward = np.block([[cosine, sine], [-sine, cosine]])
    inverse = np.block([[cosine, -sine], [sine, cosine]])
    offsets = np.arange(WIN, dtype=np.float32) - WIN // 2
    ones = np.ones(WIN, np.float32)
    square = offsets * offsets - np.mean(offsets * offsets)
    pairs = [(ones, ones), (offsets, ones), (ones, offsets), (square, ones), (ones, square), (offsets, offsets)]
    basis = np.zeros((6, 8, 128), np.float32)
    for e, (p, q) in enumerate(pairs):
        func = p[:, None] * q[None, :]
        func = func / np.sqrt(np.sum(func * func))
        for j in range(2 * BLOCKS):
            basis[e, :WIN, 8 * j : 8 * j + WIN] = func
    gather = np.zeros((128, 128), np.float32)
    for j in range(2 * BLOCKS):
        gather[8 * j : 8 * j + 8, j] = 1.0
    spread = np.zeros((LANES, 128), np.float32)
    for j in range(2 * BLOCKS):
        spread[64 * j : 64 * j + 128, j] = 1.0
    low = lambda v: v.astype(ml_dtypes.bfloat16)
    return low(first), low(nyquist), low(forward), low(inverse), low(last), basis, gather, spread


def dot(a, b, precision=None):
    return lax.dot_general(a, b, (((1,), (0,)), ((), ())), precision=precision, preferred_element_type=F32)


def row_transform(x, first_ref, nyquist_ref, real_ref, imag_ref, rows):
    for b in range(BLOCKS):
        out = dot(x[:, 128 * b : 128 * b + 256], first_ref[...])
        real_ref[rows, 128 * b : 128 * b + 128] = out[:, :128].astype(BF16)
        imag_ref[rows, 128 * b : 128 * b + 128] = out[:, 128:].astype(BF16)
    b = BLOCKS
    real_ref[rows, 128 * b : 128 * b + 128] = dot(x, nyquist_ref[...]).astype(BF16)
    imag_ref[rows, 128 * b : 128 * b + 128] = jnp.zeros((x.shape[0], 128), BF16)


def square_sums(x, sums_ref, strip):
    x = x.astype(F32)
    sums_ref[pl.ds(strip, 1), :] = jnp.sum(x * x, axis=0, keepdims=True)


def column_transform(real_ref, imag_ref, start, pair, forward_ref):
    lanes = slice(256 * pair, 256 * pair + 256)
    data = jnp.concatenate([real_ref[pl.ds(start, 128), lanes], imag_ref[pl.ds(start, 128), lanes]], 0)
    return dot(forward_ref[...], data).astype(BF16)


def kernel(peaks_ref, own_ref, next_ref, first_ref, nyquist_ref, forward_ref, inverse_ref, last_ref,
           basis_ref, gather_ref, spread_ref, out_ref,
           own_re, own_im, next_re, next_im, own_sums, next_sums, back_re, back_im, surface, windows, peak_rows):
    def first_pass(strip, carry):
        rows = pl.ds(pl.multiple_of(strip * STRIDE, STRIDE), STRIDE)
        for x_ref, re, im, sums in ((own_ref, own_re, own_im, own_sums), (next_ref, next_re, next_im, next_sums)):
            x = x_ref[rows, :]
            square_sums(x, sums, strip)
            row_transform(x, first_ref, nyquist_ref, re, im, rows)
        return carry

    lax.fori_loop(0, ROWS // STRIDE, first_pass, 0)
    lane = lax.broadcasted_iota(jnp.int32, (128, 128), 1)
    slot = lax.rem(lane, HALF) == 0
    lane8 = lax.broadcasted_iota(jnp.int32, (8, 128), 1) // 8

    def patch_row(i, carry):
        start = pl.multiple_of(i * STRIDE, STRIDE)
        for pair in range(PAIRS):
            a = column_transform(own_re, own_im, start, pair, forward_ref).astype(F32)
            b = column_transform(next_re, next_im, start, pair, forward_ref).astype(F32)
            ar, ai, br, bi = a[:128], a[128:], b[:128], b[128:]
            cross = jnp.concatenate([(ar * br + ai * bi).astype(BF16), (ar * bi - ai * br).astype(BF16)], 0)
            back = dot(inverse_ref[...], cross)
            lanes = slice(256 * pair, 256 * pair + 256)
            back_re[:, lanes] = back[:128]
            back_im[:, lanes] = back[128:]
        extra = back_re[:, 128 * BLOCKS : 128 * BLOCKS + 128]
        for b in range(BLOCKS):
            lanes = slice(128 * b, 128 * b + 128)
            moved = extra if b == 0 else pltpu.roll(extra, 128 - b, 1)
            imag = jnp.where(slot, moved, back_im[:, lanes]).astype(BF16)
            data = jnp.concatenate([back_re[:, lanes].astype(BF16), imag], 1)
            out = dot(data, last_ref[...])
            for w in range(2):
                part = out[:, 128 * w : 128 * w + 128]
                j = 2 * b + w
                surface[j, 8:136, :] = part
                surface[j, 0:8, :] = part[120:]
                surface[j, 136:144, :] = part[:8]
                peak_rows[j, pl.ds(i, 1), :] = jnp.max(jnp.abs(part), axis=0, keepdims=True)
        held = jnp.zeros((8, 128), F32)
        for j in range(2 * BLOCKS):
            dy = peaks_ref[i, 0, j]
            dx = peaks_ref[i, 1, j]
            piece = surface[j, pl.ds(dy + 6, 8), :]
            shift = lax.rem(8 * j + 2 + 128 - dx, 128)
            held = jnp.where(lane8 == j, pltpu.roll(piece, shift, 1), held)
        windows[i] = held
        return carry

    lax.fori_loop(0, 10, patch_row, 0)
    finish(windows, peak_rows, own_sums, next_sums, basis_ref, gather_ref, spread_ref, out_ref)


def finish(windows, peak_rows, own_sums, next_sums, basis_ref, gather_ref, spread_ref, out_ref):
    high = lax.Precision.HIGHEST
    energy = []
    for sums in (own_sums, next_sums):
        joined = sums[0:10, :] + sums[1:11, :]
        energy.append(dot(joined, spread_ref[...], high) / float(PATCH * PATCH))
    scale = float(PATCH) ** 3 * jnp.sqrt((energy[0] + 1e-05) * (energy[1] + 1e-05))
    lane = lax.broadcasted_iota(jnp.int32, (10, 128), 1)
    peak = jnp.zeros((10, 128), F32)
    for j in range(2 * BLOCKS):
        peak = jnp.where(lane == j, jnp.max(peak_rows[j, 0:10, :], axis=1, keepdims=True), peak)
    height = peak / scale + 1e-05
    for e in range(6):
        rows = jnp.sum(windows[...] * basis_ref[e][None], axis=1)
        value = dot(rows, gather_ref[...], high) / scale / height
        out_ref[e, :, 0, :] = value[:, :10]


def correlate(peaks, own, following):
    tables = host_tables()
    vmem = pl.BlockSpec(memory_space=pltpu.VMEM)
    return pl.pallas_call(
        kernel,
        out_shape=jax.ShapeDtypeStruct((6, 10, 1, 10), F32),
        in_specs=[pl.BlockSpec(memory_space=pltpu.SMEM)] + [vmem] * (2 + len(tables)),
        out_specs=vmem,
        scratch_shapes=[
            pltpu.VMEM((ROWS, LANES), BF16),
            pltpu.VMEM((ROWS, LANES), BF16),
            pltpu.VMEM((ROWS, LANES), BF16),
            pltpu.VMEM((ROWS, LANES), BF16),
            pltpu.VMEM((16, LANES), F32),
            pltpu.VMEM((16, LANES), F32),
            pltpu.VMEM((128, LANES), F32),
            pltpu.VMEM((128, LANES), F32),
            pltpu.VMEM((10, 144, 128), F32),
            pltpu.VMEM((10, 8, 128), F32),
            pltpu.VMEM((10, 16, 128), F32),
        ],
        compiler_params=pltpu.CompilerParams(vmem_limit_bytes=56 * 1024 * 1024),
    )(peaks, own, following, *[jnp.asarray(t) for t in tables])


def passed_along(value, axis, steps):
    count = lax.axis_size(axis)
    initial, last = (max(0, -steps), min(count, count - steps))
    return lax.ppermute(value, axis, [(source, source + steps) for source in range(initial, last)])


def body(sections, peaks, valid):
    tile = sections[0]
    lower = passed_along(tile[:STRIDE, :], "gy", -1)
    taller = jnp.concatenate([tile, lower], 0)
    beside = passed_along(taller[:, :STRIDE], "gx", -1)
    extended = jnp.concatenate([taller, beside, jnp.zeros((ROWS, LANES - ROWS), BF16)], 1)
    following = passed_along(extended, "gz", -1)
    out = correlate(jnp.transpose(peaks, (0, 2, 1, 3))[0], extended, following)
    return jnp.transpose(out, (2, 0, 1, 3)) * valid[:, None].astype(F32)


def solution(mesh):
    in_specs = (P("gz", "gy", "gx"), P("gz", None, "gy", "gx"), P("gz", "gy", "gx"))
    out_specs = P("gz", None, "gy", "gx")
    return jax.shard_map(body, mesh=mesh, in_specs=in_specs, out_specs=out_specs, check_vma=False)
```

time: 197 us -> 67.2 us (0.34)
  local copies, waits for them, and re-layouts: 49.7 us -> 2.08 us
  other arithmetic: 44.9 us -> 2.53 us
  loops' own time: 30.1 us -> 0 us
  matrix products: 27.9 us -> 0 us
  Pallas kernels: 0 us -> 20.5 us
    another operation x1 -> x0, loops' own time: 30.1 us -> none  [body(): result = lax.map(one_row, jnp.arange(patch_rows, dtype=jnp.int32))]
    dot_general x70 -> x0, matrix products: 27.9 us -> none  [the longest x10 5.67 us: correlate_row(): jnp.einsum('cnjm,km->cnjk', patches, first_table, preferred_element_type=...]
    pallas_call x0 -> x1, Pallas kernels: none -> 20.5 us  [correlate(): pl.pallas_call(kernel, out_shape=jax.ShapeDtypeStruct((6, 10, 1, 10), F32...]
    dynamic_slice x20 -> x0, local copies, waits for them, and re-layouts: 18.7 us -> none  [the longest x10 12.8 us: one_row(): block = lax.dynamic_slice_in_dim(stacked, index * STRIDE, PATCH, axis=1)]
    reduce_sum x30 -> x0, other arithmetic: 12.9 us -> none  [the longest x10 6.05 us: fit_basis(): square = offsets * offsets - jnp.mean(offsets * offsets)]
    convert_element_type x50 -> x1, other arithmetic: 11.2 us -> 0.01 us  [body(): return jnp.transpose(out, (2, 0, 1, 3)) * valid[:, None].astype(F32)]
    neg x30 -> x0, other arithmetic: 8.02 us -> none  [correlate_row(): first_table = jnp.concatenate([cosine, -sine], 0)]
    reshape x10 -> x0, local copies, waits for them, and re-layouts: 7.85 us -> none  [correlate_row(): segment_one.reshape(count, length, tiles, 2, length)]
where the time goes in v1:
time: 67.2 us; the launch traced here: 66.9 us
  waiting for transfers between devices  28.4 us (42%)
  Pallas kernels  20.5 us (31%)
  starting transfers between devices  13.3 us (20%)
  other arithmetic  2.53 us (4%)
  local copies, waits for them, and re-layouts  2.08 us (3%)
    ppermute x3, waiting for transfers between devices, passed_along(): lax.ppermute(value, axis, [(source, source + steps) for source in range(i...  28.4 us
    pallas_call x1, Pallas kernels, correlate(): pl.pallas_call(kernel, out_shape=jax.ShapeDtypeStruct((6, 10, 1, 10), F32...  20.5 us
    ppermute x3, starting transfers between devices, passed_along(): lax.ppermute(value, axis, [(source, source + steps) for source in range(i...  13.3 us
    mul x1, other arithmetic, body(): return jnp.transpose(out, (2, 0, 1, 3)) * valid[:, None].astype(F32)  1.39 us
  transfers between devices with their start and end apart: 3, of which 3 were waited for; matrix products, arithmetic and copies ran while one was open for 0% of the time, Pallas kernels for 0%

profile of v1, /device:TPU:9, one launch (start us, length us, event | category | flops | bytes accessed | tf_op | source)
XLA Modules:
  0.0 66.9 jit_solution(392195777587775940)
XLA Ops:
  0.0 0.0 copy-start.1
  0.0 1.0 %slice_bitcast_fusion = bf16[64,640]{1,0:T(8,128)(2,1)S(1)} fusion(bf16[1,640,640]{2,1,0:T(8,128)(2,1)} %param.11), kind=kLoop, calls=%fused_computation.2 | loop fusion | bytes 163840 | tf_op jit(solution)/shard_map/slice | solution.py:203
  1.0 1.3 %collective-permute-start = (bf16[64,640]{1,0:T(8,128)(2,1)S(1)}, bf16[64,640]{1,0:T(8,128)(2,1)S(1)}, u32[]{:S(2)}, u32[]{:S(2)}) collective-permute-start(bf16[64,640]{1,0:T(8,128)(2,1)S(1)} %slice_bitcast_fusion), channel_id=1, source_target_pairs={{1,0},{2,1},{3,2},{5,4},{6,5},{7,6},{9,8},{10,9},{11,10},{13,12},{... | collective-permute-start | bytes 245768 | tf_op jit(solution)/shard_map/ppermute | solution.py:198
  2.3 3.9 %collective-permute-done = bf16[64,640]{1,0:T(8,128)(2,1)S(1)} collective-permute-done((bf16[64,640]{1,0:T(8,128)(2,1)S(1)}, bf16[64,640]{1,0:T(8,128)(2,1)S(1)}, u32[]{:S(2)}, u32[]{:S(2)}) %collective-permute-start) | collective-permute-done | bytes 81952 | tf_op jit(solution)/shard_map/ppermute | solution.py:198
  6.1 0.9 %pad_maximum_fusion = bf16[704,64]{1,0:T(8,128)(2,1)S(1)} fusion(bf16[64,640]{1,0:T(8,128)(2,1)S(1)} %collective-permute-done, bf16[640,640]{1,0:T(8,128)(2,1)} %bitcast.10), kind=kLoop, calls=%fused_computation.1 | loop fusion | flops 180224 | bytes 991232 | tf_op jit(solution)/shard_map/concatenate | solution.py:204
  7.1 3.7 %collective-permute-start.1 = (bf16[704,64]{1,0:T(8,128)(2,1)S(1)}, bf16[704,64]{1,0:T(8,128)(2,1)S(1)}, u32[]{:S(2)}, u32[]{:S(2)}) collective-permute-start(bf16[704,64]{1,0:T(8,128)(2,1)S(1)} %pad_maximum_fusion), channel_id=1, source_target_pairs={{4,0},{8,4},{12,8},{5,1},{9,5},{13,9},{6,2},{10,6},{14,10},{7,3},{... | collective-permute-start | bytes 270344 | tf_op jit(solution)/shard_map/ppermute | solution.py:198
  10.8 0.1 pad.3.clone
  10.9 0.0 copy-start.3
  10.9 5.0 %collective-permute-done.1 = bf16[704,64]{1,0:T(8,128)(2,1)S(1)} collective-permute-done((bf16[704,64]{1,0:T(8,128)(2,1)S(1)}, bf16[704,64]{1,0:T(8,128)(2,1)S(1)}, u32[]{:S(2)}, u32[]{:S(2)}) %collective-permute-start.1) | collective-permute-done | bytes 90144 | tf_op jit(solution)/shard_map/ppermute | solution.py:198
  15.9 0.0 copy-done.1
  15.9 0.2 maximum_maximum_fusion.own_ref
  16.1 0.0 copy-start
  16.1 8.3 %collective-permute-start.2 = (bf16[704,768]{1,0:T(8,128)(2,1)S(1)}, bf16[704,768]{1,0:T(8,128)(2,1)S(1)}, u32[]{:S(2)}, u32[]{:S(2)}) collective-permute-start(bf16[704,768]{1,0:T(8,128)(2,1)S(1)} %maximum_maximum_fusion.own_ref), channel_id=1, source_target_pairs={{16,0},{32,16},{48,32},{64,48},{80,64},{96,80},{112,96},{128,112},... | collective-permute-start | bytes 3244040 | tf_op jit(solution)/shard_map/ppermute | solution.py:198
  24.4 0.0 copy-done.3
  24.4 19.5 %collective-permute-done.2.next_ref = bf16[704,768]{1,0:T(8,128)(2,1)S(1)} collective-permute-done((bf16[704,768]{1,0:T(8,128)(2,1)S(1)}, bf16[704,768]{1,0:T(8,128)(2,1)S(1)}, u32[]{:S(2)}, u32[]{:S(2)}) %collective-permute-start.2) | collective-permute-done | bytes 1081376 | tf_op jit(solution)/shard_map/ppermute | solution.py:198
  43.9 0.0 copy-start.2
  43.9 0.0 copy-done
  44.0 1.0 %copy-done.2 = bf16[704,768]{1,0:T(8,128)(2,1)} copy-done((bf16[704,768]{1,0:T(8,128)(2,1)}, bf16[704,768]{1,0:T(8,128)(2,1)S(1)}, u32[]{:S(2)}) %copy-start.2) | copy-done | bytes 1081368
  45.0 20.5 %shard_map.109 = f32[6,10,1,10]{3,2,1,0:T(1,128)} custom-call(s32[10,2,10]{2,1,0:T(2,128)} %bitcast.12, bf16[704,768]{1,0:T(8,128)(2,1)} %copy-done, bf16[704,768]{1,0:T(8,128)(2,1)} %copy-done.2, bf16[256,256]{1,0:T(8,128)(2,1)} %constant.18.clone.first_ref, bf16[768,128]{1,0:T(8,128)(2,1)} %constant.19.clone.nyquist_ref, ...), custom_call_target="tpu_custom_call" | custom-call | tf_op jit(solution)/shard_map/pallas_call | solution.py:173
  65.5 1.4 %bitcast_multiply_fusion = f32[1,6,10,10]{3,0,2,1:T(1,128)} fusion(f32[6,10,1,10]{3,2,1,0:T(1,128)} %shard_map.109, f32[10,10]{1,0:T(8,128)S(1)} %fusion), kind=kLoop, calls=%fused_computation.3 | loop fusion | flops 600 | bytes 5200 | tf_op jit(solution)/shard_map/mul | solution.py:209
  (2 shorter events, 0.0 us)
Async XLA Ops:
  0.0 15.9 %copy-start.1 = (bf16[1,640,640]{2,1,0:T(8,128)(2,1)S(1)}, bf16[1,640,640]{2,1,0:T(8,128)(2,1)}, u32[]{:S(2)}) copy-start(bf16[1,640,640]{2,1,0:T(8,128)(2,1)} %param.11) | copy-start | bytes 2457604
  1.0 5.2 %collective-permute-start = (bf16[64,640]{1,0:T(8,128)(2,1)S(1)}, bf16[64,640]{1,0:T(8,128)(2,1)S(1)}, u32[]{:S(2)}, u32[]{:S(2)}) collective-permute-start(bf16[64,640]{1,0:T(8,128)(2,1)S(1)} %slice_bitcast_fusion), channel_id=1, source_target_pairs={{1,0},{2,1},{3,2},{5,4},{6,5},{7,6},{9,8},{10,9},{11,10},{13,12},{... | collective-permute-start | bytes 245768 | tf_op jit(solution)/shard_map/ppermute | solution.py:198
  7.1 8.8 %collective-permute-start.1 = (bf16[704,64]{1,0:T(8,128)(2,1)S(1)}, bf16[704,64]{1,0:T(8,128)(2,1)S(1)}, u32[]{:S(2)}, u32[]{:S(2)}) collective-permute-start(bf16[704,64]{1,0:T(8,128)(2,1)S(1)} %pad_maximum_fusion), channel_id=1, source_target_pairs={{4,0},{8,4},{12,8},{5,1},{9,5},{13,9},{6,2},{10,6},{14,10},{7,3},{... | collective-permute-start | bytes 270344 | tf_op jit(solution)/shard_map/ppermute | solution.py:198
  10.9 13.5 %copy-start.3 = (s32[1,10,10]{2,0,1:T(1,128)S(1)}, s32[1,10,10]{2,0,1:T(1,128)}, u32[]{:S(2)}) copy-start(s32[1,10,10]{2,0,1:T(1,128)} %param.13) | copy-start | bytes 1204
  16.1 27.8 %copy-start = (bf16[704,768]{1,0:T(8,128)(2,1)}, bf16[704,768]{1,0:T(8,128)(2,1)S(1)}, u32[]{:S(2)}) copy-start(bf16[704,768]{1,0:T(8,128)(2,1)S(1)} %maximum_maximum_fusion.own_ref) | copy-start | bytes 3244036
  16.1 27.8 %collective-permute-start.2 = (bf16[704,768]{1,0:T(8,128)(2,1)S(1)}, bf16[704,768]{1,0:T(8,128)(2,1)S(1)}, u32[]{:S(2)}, u32[]{:S(2)}) collective-permute-start(bf16[704,768]{1,0:T(8,128)(2,1)S(1)} %maximum_maximum_fusion.own_ref), channel_id=1, source_target_pairs={{16,0},{32,16},{48,32},{64,48},{80,64},{96,80},{112,96},{128,112},... | collective-permute-start | bytes 3244040 | tf_op jit(solution)/shard_map/ppermute | solution.py:198
  43.9 1.0 %copy-start.2 = (bf16[704,768]{1,0:T(8,128)(2,1)}, bf16[704,768]{1,0:T(8,128)(2,1)S(1)}, u32[]{:S(2)}) copy-start(bf16[704,768]{1,0:T(8,128)(2,1)S(1)} %collective-permute-done.2.next_ref) | copy-start | bytes 3244036

commit v2 on v1

v2 whole, which is shorter than its diff:
```python
import functools
import math

import jax
import jax.numpy as jnp
import ml_dtypes
import numpy as np
from jax import lax
from jax.experimental import pallas as pl
from jax.experimental.pallas import tpu as pltpu
from jax.sharding import PartitionSpec as P

PATCH = 128
STRIDE = 64
WIN = 5
HALF = 64
ROWS = 704
LANES = 768
BLOCKS = 5
PAIRS = 3
CHUNKS = 6
PART_ROWS = CHUNKS * STRIDE
F32 = jnp.float32
BF16 = jnp.bfloat16


def host_tables():
    index = np.arange(PATCH)
    phase = ((index[:, None] * index[None, :]) % PATCH).astype(np.float32) * np.float32(
        2.0 * math.pi / PATCH
    )
    rounded = lambda v: v.astype(ml_dtypes.bfloat16).astype(np.float32)
    cosine, sine = rounded(np.cos(phase)), rounded(np.sin(phase))
    first = np.zeros((256, 256), np.float32)
    last = np.zeros((256, 256), np.float32)
    weight = np.where(np.arange(HALF) == 0, 1.0, 2.0).astype(np.float32)
    for w in range(2):
        rows = slice(64 * w, 64 * w + 128)
        real, imag = slice(64 * w, 64 * w + 64), slice(128 + 64 * w, 192 + 64 * w)
        lags = slice(128 * w, 128 * w + 128)
        first[rows, real] = cosine[:HALF].T
        first[rows, imag] = -sine[:HALF].T
        first[rows, 128 + 64 * w] = 0.0
        last[real, lags] = (cosine[:, :HALF] * weight).T
        last[imag, lags] = (-sine[:, :HALF] * weight).T
        last[128 + 64 * w, lags] = cosine[:, HALF]
    nyquist = np.zeros((LANES, 128), np.float32)
    for b in range(BLOCKS):
        for w in range(2):
            start = 128 * b + 64 * w
            nyquist[start : start + 128, b + 64 * w] = cosine[HALF]
    forward = np.block([[cosine, sine], [-sine, cosine]])
    inverse = np.stack([np.block([[cosine, sine], [sine, -cosine]]), np.block([[cosine, -sine], [sine, cosine]])])
    offsets = np.arange(WIN, dtype=np.float32) - WIN // 2
    ones = np.ones(WIN, np.float32)
    square = offsets * offsets - np.mean(offsets * offsets)
    pairs = [(ones, ones), (offsets, ones), (ones, offsets), (square, ones), (ones, square), (offsets, offsets)]
    basis = np.zeros((6, 8, 128), np.float32)
    for e, (p, q) in enumerate(pairs):
        func = p[:, None] * q[None, :]
        func = func / np.sqrt(np.sum(func * func))
        for j in range(2 * BLOCKS):
            basis[e, :WIN, 8 * j : 8 * j + WIN] = func
    gather = np.zeros((128, 128), np.float32)
    for j in range(2 * BLOCKS):
        gather[8 * j : 8 * j + 8, j] = 1.0
    spread = np.zeros((LANES, 128), np.float32)
    for j in range(2 * BLOCKS):
        spread[64 * j : 64 * j + 128, j] = 1.0
    low = lambda v: v.astype(ml_dtypes.bfloat16)
    return low(first), low(nyquist), low(forward), low(inverse), low(last), basis, gather, spread


def dot(a, b, precision=None):
    return lax.dot_general(a, b, (((1,), (0,)), ((), ())), precision=precision, preferred_element_type=F32)


def row_transform(x, first_ref, nyquist_ref, real_ref, imag_ref, rows):
    for b in range(BLOCKS):
        out = dot(x[:, 128 * b : 128 * b + 256], first_ref[...])
        real_ref[rows, 128 * b : 128 * b + 128] = out[:, :128].astype(BF16)
        imag_ref[rows, 128 * b : 128 * b + 128] = out[:, 128:].astype(BF16)
    b = BLOCKS
    real_ref[rows, 128 * b : 128 * b + 128] = dot(x, nyquist_ref[...]).astype(BF16)
    imag_ref[rows, 128 * b : 128 * b + 128] = jnp.zeros((x.shape[0], 128), BF16)


def square_sums(x, sums_ref, strip):
    x = x.astype(F32)
    sums_ref[pl.ds(strip, 1), :] = jnp.sum(x * x, axis=0, keepdims=True)


def column_transform(real_ref, imag_ref, start, pair, forward_ref):
    lanes = slice(256 * pair, 256 * pair + 256)
    data = jnp.concatenate([real_ref[pl.ds(start, 128), lanes], imag_ref[pl.ds(start, 128), lanes]], 0)
    return dot(forward_ref[...], data).astype(BF16)


MAIN = 640
BEFORE, AFTER = 0, 1


class Place:
    def __init__(self):
        self.at = {name: lax.axis_index(name) for name in ("gz", "gx", "gy")}
        self.size = {name: lax.axis_size(name) for name in ("gz", "gx", "gy")}

    def there(self, step):
        inside = None
        for name, move in zip(("gz", "gx", "gy"), step):
            if move:
                ok = self.at[name] + move < self.size[name] if move > 0 else self.at[name] + move >= 0
                inside = ok if inside is None else jnp.logical_and(inside, ok)
        return inside

    def device(self, step):
        return {name: self.at[name] + move for name, move in zip(("gz", "gx", "gy"), step)}


def back(step):
    return tuple(-move for move in step)


def kernel(tile_ref, peaks_ref, first_hbm, nyquist_hbm, forward_hbm, inverse_hbm, last_hbm, basis_hbm, gather_hbm, spread_hbm,
           out_ref,
           own, other, first_ref, nyquist_ref, forward_ref, inverse_ref, last_ref, basis_ref, gather_ref, spread_ref,
           own_re, own_im, other_re, other_im, spectra, own_sums, other_sums, back_re, back_im, surface, windows, peak_rows,
           result, returned, far_peaks, peaks, local_sems, send_sems, recv_sems):
    place = Place()
    tables = [(first_hbm, first_ref), (nyquist_hbm, nyquist_ref), (forward_hbm, forward_ref), (inverse_hbm, inverse_ref),
              (last_hbm, last_ref), (basis_hbm, basis_ref), (gather_hbm, gather_ref), (spread_hbm, spread_ref)]
    main, edge = pl.ds(0, MAIN), pl.ds(MAIN, 128)
    tile_copy = pltpu.make_async_copy(tile_ref, own.at[pl.ds(0, MAIN), main], local_sems.at[0])
    local = [pltpu.make_async_copy(peaks_ref.at[pl.ds(0, 5)], peaks.at[AFTER], local_sems.at[1])]
    local += [pltpu.make_async_copy(a, b, local_sems.at[2 + n]) for n, (a, b) in enumerate(tables)]
    tile_copy.start()
    for copy in local:
        copy.start()

    top = pl.ds(0, STRIDE)
    low = pl.ds(MAIN, STRIDE)
    left = pl.ds(0, 128)
    copies = [
        ((0, -1, 0), tile_ref.at[:, left], own.at[pl.ds(0, MAIN), edge]),
        ((0, 0, -1), tile_ref.at[top, :], own.at[low, main]),
        ((0, -1, -1), tile_ref.at[top, left], own.at[low, edge]),
        ((1, 0, 0), peaks_ref.at[pl.ds(5, 5)], far_peaks),
        ((-1, 0, 0), result, returned),
    ]
    early, ret = len(copies) - 1, len(copies) - 1
    parts = {}
    for c in range(CHUNKS):
        rows = pl.ds(STRIDE * c, STRIDE)
        for part in (BEFORE, AFTER):
            for columns, source_columns, shift in ((main, main, 0), (edge, left, -1)):
                move = -1 if part == AFTER else 1
                if part == BEFORE and c == CHUNKS - 1:
                    step, source = (move, shift, -1), top
                else:
                    step = (move, shift, 0)
                    source = rows if part == AFTER else pl.ds(MAIN - PART_ROWS + STRIDE + STRIDE * c, STRIDE)
                parts[c, part, shift] = len(copies)
                copies.append((step, tile_ref.at[source, source_columns], other.at[part, rows, columns]))

    def remote(n):
        step, source, destination = copies[n]
        return pltpu.make_async_remote_copy(
            src_ref=source, dst_ref=destination, send_sem=send_sems.at[n], recv_sem=recv_sems.at[n],
            device_id=place.device(step), device_id_type=pl.DeviceIdType.MESH,
        )

    def wait_for(n):
        pl.when(place.there(back(copies[n][0])))(lambda: remote(n).wait_recv())

    @pl.when(place.at["gy"] == place.size["gy"] - 1)
    def _():
        own[MAIN:ROWS, :] = jnp.zeros((STRIDE, LANES), BF16)
        other[BEFORE, PART_ROWS - STRIDE :, :] = jnp.zeros((STRIDE, LANES), BF16)

    @pl.when(place.at["gx"] == place.size["gx"] - 1)
    def _():
        own[:, MAIN:] = jnp.zeros((ROWS, LANES - MAIN), BF16)
        for part in (BEFORE, AFTER):
            other[part, :, MAIN:] = jnp.zeros((PART_ROWS, LANES - MAIN), BF16)

    @pl.when(place.at["gz"] == place.size["gz"] - 1)
    def _():
        other[AFTER] = jnp.zeros((PART_ROWS, LANES), BF16)
        returned[...] = jnp.zeros_like(returned)

    @pl.when(place.at["gz"] == 0)
    def _():
        other[BEFORE] = jnp.zeros((PART_ROWS, LANES), BF16)
        far_peaks[...] = jnp.zeros_like(far_peaks)

    barrier = pltpu.get_barrier_semaphore()
    steps = sorted({step for step, _, _ in copies})
    for step in steps:
        @pl.when(place.there(back(step)))
        def _():
            pl.semaphore_signal(barrier, inc=1, device_id=place.device(back(step)), device_id_type=pl.DeviceIdType.MESH)
    pl.semaphore_wait(barrier, sum(place.there(step).astype(jnp.int32) for step in steps))
    for n in range(len(copies)):
        if n != ret:
            pl.when(place.there(copies[n][0]))(lambda: remote(n).start())

    tile_copy.wait()
    for copy in local:
        copy.wait()
    for n in range(3):
        wait_for(n)

    def own_rows(strip, carry):
        rows = pl.ds(pl.multiple_of(strip * STRIDE, STRIDE), STRIDE)
        x = own[rows, :]
        square_sums(x, own_sums, strip)
        row_transform(x, first_ref, nyquist_ref, own_re, own_im, rows)
        return carry

    lax.fori_loop(0, ROWS // STRIDE, own_rows, 0)

    def own_spectra(i, carry):
        start = pl.multiple_of(i * STRIDE, STRIDE)
        for pair in range(PAIRS):
            spectra[i, pair] = column_transform(own_re, own_im, start, pair, forward_ref)
        return carry

    lax.fori_loop(0, 10, own_spectra, 0)
    wait_for(3)
    far = pltpu.make_async_copy(far_peaks, peaks.at[BEFORE], local_sems.at[1])
    far.start()
    far.wait()

    lane = lax.broadcasted_iota(jnp.int32, (128, 128), 1)
    slot = lax.rem(lane, HALF) == 0
    lane8 = lax.broadcasted_iota(jnp.int32, (8, 128), 1) // 8

    def wait_chunk(c, part):
        for shift in (0, -1):
            wait_for(parts[c, part, shift])

    def other_rows(c, part):
        rows = pl.ds(pl.multiple_of(c * STRIDE, STRIDE), STRIDE)
        x = other[part, rows, :]
        square_sums(x, other_sums.at[part], c)
        row_transform(x, first_ref, nyquist_ref, other_re.at[part], other_im.at[part], rows)

    def patch_row(i, part):
        start = pl.multiple_of(i * STRIDE, STRIDE)
        row = jnp.where(part == BEFORE, 5, 0) + i
        for pair in range(PAIRS):
            a = spectra[row, pair].astype(F32)
            b = column_transform(other_re.at[part], other_im.at[part], start, pair, forward_ref).astype(F32)
            ar, ai, br, bi = a[:128], a[128:], b[:128], b[128:]
            cross = jnp.concatenate([(ar * br + ai * bi).astype(BF16), (ar * bi - ai * br).astype(BF16)], 0)
            turned = dot(inverse_ref[part], cross)
            lanes = slice(256 * pair, 256 * pair + 256)
            back_re[:, lanes] = turned[:128]
            back_im[:, lanes] = turned[128:]
        extra = back_re[:, 128 * BLOCKS : 128 * BLOCKS + 128]
        for b in range(BLOCKS):
            lanes = slice(128 * b, 128 * b + 128)
            moved = extra if b == 0 else pltpu.roll(extra, 128 - b, 1)
            imag = jnp.where(slot, moved, back_im[:, lanes]).astype(BF16)
            data = jnp.concatenate([back_re[:, lanes].astype(BF16), imag], 1)
            out = dot(data, last_ref[...])
            for w in range(2):
                piece = out[:, 128 * w : 128 * w + 128]
                j = 2 * b + w
                surface[j, 8:136, :] = piece
                surface[j, 0:8, :] = piece[120:]
                surface[j, 136:144, :] = piece[:8]
                peak_rows[part, j, pl.ds(i, 1), :] = jnp.max(jnp.abs(piece), axis=0, keepdims=True)
        held = jnp.zeros((8, 128), F32)
        for j in range(2 * BLOCKS):
            dy = peaks[part, i, 0, j]
            dx = peaks[part, i, 1, j]
            piece = surface[j, pl.ds(dy + 6, 8), :]
            shift = lax.rem(8 * j + 2 + 128 - dx, 128)
            held = jnp.where(lane8 == j, pltpu.roll(piece, shift, 1), held)
        windows[part, i] = held

    def finish(part):
        high = lax.Precision.HIGHEST
        first = 5 if part == BEFORE else 0
        joined = [own_sums[first : first + 5, :] + own_sums[first + 1 : first + 6, :],
                  other_sums[part, 0:5, :] + other_sums[part, 1:6, :]]
        energy = [dot(sums, spread_ref[...], high) / float(PATCH * PATCH) for sums in joined]
        scale = float(PATCH) ** 3 * jnp.sqrt((energy[0] + 1e-05) * (energy[1] + 1e-05))
        lane5 = lax.broadcasted_iota(jnp.int32, (5, 128), 1)
        peak = jnp.zeros((5, 128), F32)
        for j in range(2 * BLOCKS):
            peak = jnp.where(lane5 == j, jnp.max(peak_rows[part, j, 0:5, :], axis=1, keepdims=True), peak)
        height = peak / scale + 1e-05
        values = []
        for e in range(6):
            rows = jnp.sum(windows[part] * basis_ref[e][None], axis=1)
            values.append(dot(rows, gather_ref[...], high) / scale / height)
        return values

    for part in (BEFORE, AFTER):
        wait_chunk(0, part)
        other_rows(0, part)

    for c in range(1, CHUNKS):
        for part in (BEFORE, AFTER):
            wait_chunk(c, part)
        def both(part, carry):
            other_rows(c, part)
            patch_row(c - 1, part)
            return carry
        lax.fori_loop(0, 2, both, 0)

    for e, value in enumerate(finish(BEFORE)):
        result[e, 0:5, :] = value
    pl.when(place.there(copies[ret][0]))(lambda: remote(ret).start())
    for e, value in enumerate(finish(AFTER)):
        out_ref[e, 0:5, 0, :] = value[:, :10]
    wait_for(ret)
    for e in range(6):
        out_ref[e, 5:10, 0, :] = returned[e, 0:5, :10]
    for n in range(len(copies)):
        pl.when(place.there(copies[n][0]))(lambda: remote(n).wait_send())


def correlate(tile, peaks):
    tables = host_tables()
    anywhere = pl.BlockSpec(memory_space=pl.ANY)
    count = 5 + 4 * CHUNKS
    return pl.pallas_call(
        kernel,
        out_shape=jax.ShapeDtypeStruct((6, 10, 1, 10), F32),
        in_specs=[anywhere] * (2 + len(tables)),
        out_specs=pl.BlockSpec(memory_space=pltpu.VMEM),
        scratch_shapes=[
            pltpu.VMEM((ROWS, LANES), BF16),
            pltpu.VMEM((2, PART_ROWS, LANES), BF16),
            *[pltpu.VMEM(t.shape, t.dtype) for t in tables],
            pltpu.VMEM((ROWS, LANES), BF16),
            pltpu.VMEM((ROWS, LANES), BF16),
            pltpu.VMEM((2, PART_ROWS, LANES), BF16),
            pltpu.VMEM((2, PART_ROWS, LANES), BF16),
            pltpu.VMEM((10, PAIRS, 256, 256), BF16),
            pltpu.VMEM((16, LANES), F32),
            pltpu.VMEM((2, 8, LANES), F32),
            pltpu.VMEM((128, LANES), F32),
            pltpu.VMEM((128, LANES), F32),
            pltpu.VMEM((10, 144, 128), F32),
            pltpu.VMEM((2, 5, 8, 128), F32),
            pltpu.VMEM((2, 10, 8, 128), F32),
            pltpu.VMEM((6, 8, 128), F32),
            pltpu.VMEM((6, 8, 128), F32),
            pltpu.VMEM((5, 2, 10), jnp.int32),
            pltpu.SMEM((2, 5, 2, 10), jnp.int32),
            pltpu.SemaphoreType.DMA((2 + len(tables),)),
            pltpu.SemaphoreType.DMA((count,)),
            pltpu.SemaphoreType.DMA((count,)),
        ],
        compiler_params=pltpu.CompilerParams(
            collective_id=0, has_side_effects=True, vmem_limit_bytes=48 * 1024 * 1024
        ),
    )(tile, peaks, *[jnp.asarray(t) for t in tables])


def body(sections, peaks, valid):
    out = correlate(sections[0], jnp.transpose(peaks, (0, 2, 1, 3))[0])
    return jnp.transpose(out, (2, 0, 1, 3)) * valid[:, None].astype(F32)


def solution(mesh):
    in_specs = (P("gz", "gy", "gx"), P("gz", None, "gy", "gx"), P("gz", "gy", "gx"))
    out_specs = P("gz", None, "gy", "gx")
    return jax.shard_map(body, mesh=mesh, in_specs=in_specs, out_specs=out_specs, check_vma=False)
```

time: 67.2 us -> 51.4 us (0.76)
  the two profiles are of different devices: /device:TPU:9 before, /device:TPU:203 now
where the time goes in v2:
time: 51.4 us; the launch traced here: 51 us
  Pallas kernels  41.3 us (80%)
  local copies, waits for them, and re-layouts  8.32 us (16%)
  other arithmetic  1.33 us (3%)
    pallas_call x1, Pallas kernels, correlate(): pl.pallas_call(kernel, out_shape=jax.ShapeDtypeStruct((6, 10, 1, 10), F32...  41.3 us
    unnamed x20, local copies, waits for them, and re-layouts  8.32 us

profile of v2, /device:TPU:203, one launch (start us, length us, event | category | flops | bytes accessed | tf_op | source)
XLA Modules:
  0.0 51.0 jit_solution(2051075958562362413)
XLA Ops:
  0.0 0.0 copy-start.8
  0.0 0.7 %fusion = f32[10,10]{1,0:T(8,128)S(1)} fusion(s32[1,10,10]{2,0,1:T(1,128)} %param.13), kind=kLoop, calls=%fused_computation.2 | loop fusion | flops 100 | bytes 800 | tf_op jit(solution)/shard_map/convert_element_type | solution.py:367
  0.7 0.1 copy-done.8
  0.8 0.0 copy-start
  0.8 1.1 %copy-done = bf16[1,640,640]{2,1,0:T(8,128)(2,1)S(1)} copy-done((bf16[1,640,640]{2,1,0:T(8,128)(2,1)S(1)}, bf16[1,640,640]{2,1,0:T(8,128)(2,1)}, u32[]{:S(2)}) %copy-start) | copy-done | bytes 819224
  1.9 0.0 copy-start.1
  1.9 1.0 %copy-done.1 = f32[768,128]{1,0:T(8,128)S(1)} copy-done((f32[768,128]{1,0:T(8,128)S(1)}, f32[768,128]{1,0:T(8,128)}, u32[]{:S(2)}) %copy-start.1) | copy-done | bytes 393240
  2.9 0.0 copy-start.2
  2.9 0.9 %copy-done.2 = bf16[2,256,256]{2,1,0:T(8,128)(2,1)S(1)} copy-done((bf16[2,256,256]{2,1,0:T(8,128)(2,1)S(1)}, bf16[2,256,256]{2,1,0:T(8,128)(2,1)}, u32[]{:S(2)}) %copy-start.2) | copy-done | bytes 262168
  3.8 0.0 copy-start.3
  3.8 0.9 %copy-done.3 = bf16[768,128]{1,0:T(8,128)(2,1)S(1)} copy-done((bf16[768,128]{1,0:T(8,128)(2,1)S(1)}, bf16[768,128]{1,0:T(8,128)(2,1)}, u32[]{:S(2)}) %copy-start.3) | copy-done | bytes 196632
  4.8 0.0 copy-start.4
  4.8 0.9 %copy-done.4 = bf16[256,256]{1,0:T(8,128)(2,1)S(1)} copy-done((bf16[256,256]{1,0:T(8,128)(2,1)S(1)}, bf16[256,256]{1,0:T(8,128)(2,1)}, u32[]{:S(2)}) %copy-start.4) | copy-done | bytes 131096
  5.7 0.0 copy-start.5
  5.7 0.9 %copy-done.5 = bf16[256,256]{1,0:T(8,128)(2,1)S(1)} copy-done((bf16[256,256]{1,0:T(8,128)(2,1)S(1)}, bf16[256,256]{1,0:T(8,128)(2,1)}, u32[]{:S(2)}) %copy-start.5) | copy-done | bytes 131096
  6.6 0.0 copy-start.6
  6.6 0.9 %copy-done.6 = bf16[256,256]{1,0:T(8,128)(2,1)S(1)} copy-done((bf16[256,256]{1,0:T(8,128)(2,1)S(1)}, bf16[256,256]{1,0:T(8,128)(2,1)}, u32[]{:S(2)}) %copy-start.6) | copy-done | bytes 131096
  7.5 0.0 copy-start.7
  7.5 0.8 %copy-done.7 = f32[128,128]{1,0:T(8,128)S(1)} copy-done((f32[128,128]{1,0:T(8,128)S(1)}, f32[128,128]{1,0:T(8,128)}, u32[]{:S(2)}) %copy-start.7) | copy-done | bytes 65560
  8.3 0.0 copy-start.9
  8.3 0.7 %copy-done.9 = s32[1,2,10,10]{3,1,2,0:T(2,128)S(1)} copy-done((s32[1,2,10,10]{3,1,2,0:T(2,128)S(1)}, s32[1,2,10,10]{3,1,2,0:T(2,128)}, u32[]{:S(2)}) %copy-start.9) | copy-done | bytes 824
  9.0 41.3 %shard_map.109 = f32[6,10,1,10]{3,2,1,0:T(1,128)S(1)} custom-call(bf16[640,640]{1,0:T(8,128)(2,1)S(1)} %bitcast.8, s32[10,2,10]{2,1,0:T(2,128)S(1)} %bitcast.9, bf16[256,256]{1,0:T(8,128)(2,1)S(1)} %copy-done.6, bf16[768,128]{1,0:T(8,128)(2,1)S(1)} %copy-done.3, bf16[256,256]{1,0:T(8,128)(2,1)S(1)} %copy-done.5, bf16[2,256,256]{2,1,0:T(8,128)(2,1)S(1)} %copy-done.2, ...), custom_call_target="tpu_custom_call" | custom-call | tf_op jit(solution)/shard_map/pallas_call | solution.py:330
  50.4 0.6 %bitcast_multiply_fusion = f32[1,6,10,10]{3,0,2,1:T(1,128)} fusion(f32[6,10,1,10]{3,2,1,0:T(1,128)S(1)} %shard_map.109, f32[10,10]{1,0:T(8,128)S(1)} %fusion), kind=kLoop, calls=%fused_computation | loop fusion | flops 600 | bytes 5200 | tf_op jit(solution)/shard_map/mul | solution.py:367
Async XLA Ops:
  0.0 0.8 %copy-start.8 = (f32[6,8,128]{2,1,0:T(8,128)S(1)}, f32[6,8,128]{2,1,0:T(8,128)}, u32[]{:S(2)}) copy-start(f32[6,8,128]{2,1,0:T(8,128)} %constant.21.clone.basis_hbm) | copy-start | bytes 73732
  0.8 1.1 %copy-start = (bf16[1,640,640]{2,1,0:T(8,128)(2,1)S(1)}, bf16[1,640,640]{2,1,0:T(8,128)(2,1)}, u32[]{:S(2)}) copy-start(bf16[1,640,640]{2,1,0:T(8,128)(2,1)} %param.11) | copy-start | bytes 2457604
  1.9 1.0 %copy-start.1 = (f32[768,128]{1,0:T(8,128)S(1)}, f32[768,128]{1,0:T(8,128)}, u32[]{:S(2)}) copy-start(f32[768,128]{1,0:T(8,128)} %constant.23.clone.spread_hbm) | copy-start | bytes 1179652
  2.9 0.9 %copy-start.2 = (bf16[2,256,256]{2,1,0:T(8,128)(2,1)S(1)}, bf16[2,256,256]{2,1,0:T(8,128)(2,1)}, u32[]{:S(2)}) copy-start(bf16[2,256,256]{2,1,0:T(8,128)(2,1)} %constant.19.clone.inverse_hbm) | copy-start | bytes 786436
  3.8 0.9 %copy-start.3 = (bf16[768,128]{1,0:T(8,128)(2,1)S(1)}, bf16[768,128]{1,0:T(8,128)(2,1)}, u32[]{:S(2)}) copy-start(bf16[768,128]{1,0:T(8,128)(2,1)} %constant.17.clone.nyquist_hbm) | copy-start | bytes 589828
  4.8 0.9 %copy-start.4 = (bf16[256,256]{1,0:T(8,128)(2,1)S(1)}, bf16[256,256]{1,0:T(8,128)(2,1)}, u32[]{:S(2)}) copy-start(bf16[256,256]{1,0:T(8,128)(2,1)} %constant.20.clone.last_hbm) | copy-start | bytes 393220
  5.7 0.9 %copy-start.5 = (bf16[256,256]{1,0:T(8,128)(2,1)S(1)}, bf16[256,256]{1,0:T(8,128)(2,1)}, u32[]{:S(2)}) copy-start(bf16[256,256]{1,0:T(8,128)(2,1)} %constant.18.clone.forward_hbm) | copy-start | bytes 393220
  6.6 0.9 %copy-start.6 = (bf16[256,256]{1,0:T(8,128)(2,1)S(1)}, bf16[256,256]{1,0:T(8,128)(2,1)}, u32[]{:S(2)}) copy-start(bf16[256,256]{1,0:T(8,128)(2,1)} %constant.16.clone.first_hbm) | copy-start | bytes 393220
  7.5 0.8 %copy-start.7 = (f32[128,128]{1,0:T(8,128)S(1)}, f32[128,128]{1,0:T(8,128)}, u32[]{:S(2)}) copy-start(f32[128,128]{1,0:T(8,128)} %constant.22.clone.gather_hbm) | copy-start | bytes 196612
  8.3 0.7 %copy-start.9 = (s32[1,2,10,10]{3,1,2,0:T(2,128)S(1)}, s32[1,2,10,10]{3,1,2,0:T(2,128)}, u32[]{:S(2)}) copy-start(s32[1,2,10,10]{3,1,2,0:T(2,128)} %param.12) | copy-start | bytes 2404

commit v3 on v2

v3 whole, which is shorter than its diff:
```python
import functools
import math

import jax
import jax.numpy as jnp
import ml_dtypes
import numpy as np
from jax import lax
from jax.experimental import pallas as pl
from jax.experimental.pallas import tpu as pltpu
from jax.sharding import PartitionSpec as P

PATCH = 128
STRIDE = 64
WIN = 5
HALF = 64
ROWS = 704
LANES = 768
BLOCKS = 5
PAIRS = 3
CHUNKS = 6
PART_ROWS = CHUNKS * STRIDE
F32 = jnp.float32
BF16 = jnp.bfloat16


def host_tables():
    index = np.arange(PATCH)
    phase = ((index[:, None] * index[None, :]) % PATCH).astype(np.float32) * np.float32(
        2.0 * math.pi / PATCH
    )
    rounded = lambda v: v.astype(ml_dtypes.bfloat16).astype(np.float32)
    cosine, sine = rounded(np.cos(phase)), rounded(np.sin(phase))
    first = np.zeros((256, 256), np.float32)
    last = np.zeros((256, 256), np.float32)
    weight = np.where(np.arange(HALF) == 0, 1.0, 2.0).astype(np.float32)
    for w in range(2):
        rows = slice(64 * w, 64 * w + 128)
        real, imag = slice(64 * w, 64 * w + 64), slice(128 + 64 * w, 192 + 64 * w)
        lags = slice(128 * w, 128 * w + 128)
        first[rows, real] = cosine[:HALF].T
        first[rows, imag] = -sine[:HALF].T
        first[rows, 128 + 64 * w] = 0.0
        last[real, lags] = (cosine[:, :HALF] * weight).T
        last[imag, lags] = (-sine[:, :HALF] * weight).T
        last[128 + 64 * w, lags] = cosine[:, HALF]
    nyquist = np.zeros((LANES, 128), np.float32)
    for b in range(BLOCKS):
        for w in range(2):
            start = 128 * b + 64 * w
            nyquist[start : start + 128, b + 64 * w] = cosine[HALF]
    forward = np.block([[cosine, sine], [-sine, cosine]])
    inverse = np.stack([np.block([[cosine, sine], [sine, -cosine]]), np.block([[cosine, -sine], [sine, cosine]])])
    offsets = np.arange(WIN, dtype=np.float32) - WIN // 2
    ones = np.ones(WIN, np.float32)
    square = offsets * offsets - np.mean(offsets * offsets)
    pairs = [(ones, ones), (offsets, ones), (ones, offsets), (square, ones), (ones, square), (offsets, offsets)]
    basis = np.zeros((6, 8, 128), np.float32)
    for e, (p, q) in enumerate(pairs):
        func = p[:, None] * q[None, :]
        func = func / np.sqrt(np.sum(func * func))
        for j in range(2 * BLOCKS):
            basis[e, :WIN, 8 * j : 8 * j + WIN] = func
    gather = np.zeros((128, 128), np.float32)
    for j in range(2 * BLOCKS):
        gather[8 * j : 8 * j + 8, j] = 1.0
    spread = np.zeros((LANES, 128), np.float32)
    for j in range(2 * BLOCKS):
        spread[64 * j : 64 * j + 128, j] = 1.0
    low = lambda v: v.astype(ml_dtypes.bfloat16)
    return low(first), low(nyquist), low(forward), low(inverse), low(last), basis, gather, spread


def dot(a, b, precision=None):
    return lax.dot_general(a, b, (((1,), (0,)), ((), ())), precision=precision, preferred_element_type=F32)


def row_transform(x, first_ref, block):
    return dot(x[:, 128 * block : 128 * block + 256], first_ref[...]).astype(BF16)


def unpack(packed):
    wide = packed.astype(F32)
    return jnp.concatenate([wide, pltpu.roll(wide, HALF, 1)], 0).astype(BF16)


def square_sums(x, sums_ref, strip):
    x = x.astype(F32)
    sums_ref[pl.ds(strip, 1), :] = jnp.sum(x * x, axis=0, keepdims=True)


def column_transform(real_ref, imag_ref, start, forward_ref):
    data = jnp.concatenate([real_ref[pl.ds(start, 128), :], imag_ref[pl.ds(start, 128), :]], 0)
    return dot(forward_ref[...], data).astype(BF16)


MAIN = 640
BEFORE, AFTER = 0, 1


class Place:
    def __init__(self):
        self.at = {name: lax.axis_index(name) for name in ("gz", "gx", "gy")}
        self.size = {name: lax.axis_size(name) for name in ("gz", "gx", "gy")}

    def there(self, step):
        inside = None
        for name, move in zip(("gz", "gx", "gy"), step):
            if move:
                ok = self.at[name] + move < self.size[name] if move > 0 else self.at[name] + move >= 0
                inside = ok if inside is None else jnp.logical_and(inside, ok)
        return inside

    def device(self, step):
        return {name: self.at[name] + move for name, move in zip(("gz", "gx", "gy"), step)}


def back(step):
    return tuple(-move for move in step)


def kernel(tile_ref, peaks_ref, first_hbm, nyquist_hbm, forward_hbm, inverse_hbm, last_hbm, basis_hbm, gather_hbm, spread_hbm,
           out_ref,
           own, other, packed, own_edge, other_edge,
           first_ref, nyquist_ref, forward_ref, inverse_ref, last_ref, basis_ref, gather_ref, spread_ref,
           own_re, own_im, other_re, other_im, spectra, own_sums, other_sums, surface, windows, peak_rows,
           result, returned, far_peaks, peaks, local_sems, send_sems, recv_sems):
    place = Place()
    tables = [(first_hbm, first_ref), (nyquist_hbm, nyquist_ref), (forward_hbm, forward_ref), (inverse_hbm, inverse_ref),
              (last_hbm, last_ref), (basis_hbm, basis_ref), (gather_hbm, gather_ref), (spread_hbm, spread_ref)]
    main = pl.ds(0, MAIN)
    tile_copy = pltpu.make_async_copy(tile_ref, own.at[main, main], local_sems.at[0])
    local = [pltpu.make_async_copy(peaks_ref.at[pl.ds(0, 5)], peaks.at[AFTER], local_sems.at[1])]
    local += [pltpu.make_async_copy(a, b, local_sems.at[2 + n]) for n, (a, b) in enumerate(tables)]
    tile_copy.start()
    for copy in local:
        copy.start()

    copies = [
        ((0, 0, -1), tile_ref.at[pl.ds(0, STRIDE), :], own.at[pl.ds(MAIN, STRIDE), main]),
        ((0, -1, 0), packed, own_edge.at[pl.ds(0, MAIN // 2)]),
        ((0, -1, -1), packed.at[pl.ds(0, 32)], own_edge.at[pl.ds(MAIN // 2, 32)]),
        ((1, 0, 0), peaks_ref.at[pl.ds(5, 5)], far_peaks),
        ((-1, 0, 0), result, returned),
    ]
    ret = len(copies) - 1
    base = len(copies)
    for c in range(CHUNKS):
        for part in (BEFORE, AFTER):
            move = -1 if part == AFTER else 1
            strip = c if part == AFTER else (5 + c) % 10
            low = -1 if part == BEFORE and c == CHUNKS - 1 else 0
            rows = pl.ds(STRIDE * c, STRIDE)
            copies.append(((move, 0, low), tile_ref.at[pl.ds(STRIDE * strip, STRIDE), :], other.at[part, rows, :]))
            copies.append(((move, -1, low), packed.at[pl.ds(32 * strip, 32)], other_edge.at[part, pl.ds(32 * c, 32)]))

    def remote(n):
        step, source, destination = copies[n]
        return pltpu.make_async_remote_copy(
            src_ref=source, dst_ref=destination, send_sem=send_sems.at[n], recv_sem=recv_sems.at[n],
            device_id=place.device(step), device_id_type=pl.DeviceIdType.MESH,
        )

    def wait_for(n):
        pl.when(place.there(back(copies[n][0])))(lambda: remote(n).wait_recv())

    @pl.when(place.at["gy"] == place.size["gy"] - 1)
    def _():
        own[MAIN:ROWS, :MAIN] = jnp.zeros((STRIDE, MAIN), BF16)
        own_edge[MAIN // 2 :, :] = jnp.zeros((32, 128), BF16)
        other[BEFORE, PART_ROWS - STRIDE :, :] = jnp.zeros((STRIDE, MAIN), BF16)
        other_edge[BEFORE, PART_ROWS // 2 - 32 :, :] = jnp.zeros((32, 128), BF16)

    @pl.when(place.at["gx"] == place.size["gx"] - 1)
    def _():
        own_edge[...] = jnp.zeros_like(own_edge)
        other_edge[...] = jnp.zeros_like(other_edge)

    @pl.when(place.at["gz"] == place.size["gz"] - 1)
    def _():
        other[AFTER] = jnp.zeros((PART_ROWS, MAIN), BF16)
        other_edge[AFTER] = jnp.zeros((PART_ROWS // 2, 128), BF16)
        returned[...] = jnp.zeros_like(returned)

    @pl.when(place.at["gz"] == 0)
    def _():
        other[BEFORE] = jnp.zeros((PART_ROWS, MAIN), BF16)
        other_edge[BEFORE] = jnp.zeros((PART_ROWS // 2, 128), BF16)
        far_peaks[...] = jnp.zeros_like(far_peaks)

    lane = lax.broadcasted_iota(jnp.int32, (128, 128), 1)
    slot = lax.rem(lane, HALF) == 0
    lane8 = lax.broadcasted_iota(jnp.int32, (8, 128), 1) // 8
    left = lax.broadcasted_iota(jnp.int32, (32, 128), 1) < HALF

    barrier = pltpu.get_barrier_semaphore()
    steps = sorted({step for step, _, _ in copies})
    for step in steps:
        @pl.when(place.there(back(step)))
        def _():
            pl.semaphore_signal(barrier, inc=1, device_id=place.device(back(step)), device_id_type=pl.DeviceIdType.MESH)
    tile_copy.wait()
    for n in range(MAIN // STRIDE):
        block = own[STRIDE * n : STRIDE * n + STRIDE, 0:128].astype(F32)
        packed[32 * n : 32 * n + 32, :] = jnp.where(left, block[:32], pltpu.roll(block[32:], HALF, 1)).astype(BF16)
    pl.semaphore_wait(barrier, sum(place.there(step).astype(jnp.int32) for step in steps))
    for n in range(len(copies)):
        if n != ret:
            pl.when(place.there(copies[n][0]))(lambda: remote(n).start())

    windows[...] = jnp.zeros_like(windows)
    peak_rows[...] = jnp.zeros_like(peak_rows)
    for copy in local:
        copy.wait()

    def keep(re, im, rows, b, out):
        re[rows, 128 * b : 128 * b + 128] = out[:, :128]
        im[rows, 128 * b : 128 * b + 128] = out[:, 128:]

    def keep_nyquist(re, im, rows, out):
        re[rows, 128 * BLOCKS :] = out
        im[rows, 128 * BLOCKS :] = jnp.zeros((out.shape[0], 128), BF16)

    for b in range(BLOCKS - 1):
        keep(own_re, own_im, slice(0, MAIN), b, row_transform(own[0:MAIN, :], first_ref, b))
    for n in range(3):
        wait_for(n)

    def own_strip(strip, carry):
        rows = pl.ds(pl.multiple_of(strip * STRIDE, STRIDE), STRIDE)
        own[rows, MAIN:] = unpack(own_edge[pl.ds(pl.multiple_of(strip * 32, 32), 32), :])
        square_sums(own[rows, :], own_sums, strip)
        return carry

    lax.fori_loop(0, ROWS // STRIDE, own_strip, 0)
    for b in range(BLOCKS - 1):
        keep(own_re, own_im, slice(MAIN, ROWS), b, row_transform(own[MAIN:ROWS, :], first_ref, b))
    keep(own_re, own_im, slice(0, ROWS), BLOCKS - 1, row_transform(own[...], first_ref, BLOCKS - 1))
    keep_nyquist(own_re, own_im, slice(0, ROWS), dot(own[...], nyquist_ref[...]).astype(BF16))

    def own_spectra(i, carry):
        for half in range(2):
            row = 5 * half + i
            spectra[row] = column_transform(own_re, own_im, pl.multiple_of(row * STRIDE, STRIDE), forward_ref)
        return carry

    lax.fori_loop(0, 5, own_spectra, 0)
    wait_for(3)
    far = pltpu.make_async_copy(far_peaks, peaks.at[BEFORE], local_sems.at[1])
    far.start()
    far.wait()

    both = (BEFORE, AFTER)

    def wait_chunk(c):
        rows = pl.ds(pl.multiple_of(c * STRIDE, STRIDE), STRIDE)
        half = pl.ds(pl.multiple_of(c * 32, 32), 32)
        for part in both:
            there = place.there((1, 0, 0)) if part == AFTER else jnp.logical_and(
                place.there((-1, 0, 0)), jnp.logical_or(c < CHUNKS - 1, place.there((0, 0, 1))))
            beside = jnp.logical_and(there, place.there((0, 1, 0)))
            n = base + 4 * c + 2 * part
            for k, (ok, ref) in enumerate(((there, other.at[part, rows, :]), (beside, other_edge.at[part, half]))):
                @pl.when(ok)
                def _():
                    pltpu.make_async_remote_copy(
                        src_ref=ref, dst_ref=ref, send_sem=send_sems.at[n + k], recv_sem=recv_sems.at[n + k],
                        device_id=place.device((0, 0, 0)), device_id_type=pl.DeviceIdType.MESH,
                    ).wait_recv()

    def other_rows(c):
        rows = pl.ds(pl.multiple_of(c * STRIDE, STRIDE), STRIDE)
        half = pl.ds(pl.multiple_of(c * 32, 32), 32)
        pieces = [jnp.concatenate([other[part, rows, :], unpack(other_edge[part, half, :])], 1) for part in both]
        x = jnp.concatenate(pieces, 0)
        for b in range(BLOCKS):
            out = row_transform(x, first_ref, b)
            for part in both:
                keep(other_re.at[part], other_im.at[part], rows, b, out[64 * part : 64 * part + 64])
        out = dot(x, nyquist_ref[...]).astype(BF16)
        for part in both:
            keep_nyquist(other_re.at[part], other_im.at[part], rows, out[64 * part : 64 * part + 64])
            square_sums(pieces[part], other_sums.at[part], c)

    def patch_rows(i):
        start = pl.multiple_of(i * STRIDE, STRIDE)
        crosses = []
        for part in both:
            a = spectra[(5 if part == BEFORE else 0) + i].astype(F32)
            b = column_transform(other_re.at[part], other_im.at[part], start, forward_ref).astype(F32)
            ar, ai, br, bi = a[:128], a[128:], b[:128], b[128:]
            crosses.append(jnp.concatenate([(ar * br + ai * bi).astype(BF16), (ar * bi - ai * br).astype(BF16)], 0))
        for part in both:
            turned = dot(inverse_ref[part], crosses[part])
            extra = turned[:128, 128 * BLOCKS :]
            for b in range(BLOCKS):
                lanes = slice(128 * b, 128 * b + 128)
                moved = extra if b == 0 else pltpu.roll(extra, 128 - b, 1)
                imag = jnp.where(slot, moved, turned[128:, lanes]).astype(BF16)
                out = dot(jnp.concatenate([turned[:128, lanes].astype(BF16), imag], 1), last_ref[...])
                for w in range(2):
                    piece = out[:, 128 * w : 128 * w + 128]
                    j = 2 * b + w
                    surface[part, j, 8:136, :] = piece
                    surface[part, j, 0:8, :] = piece[120:]
                    surface[part, j, 136:144, :] = piece[:8]
                    peak_rows[part, j, pl.ds(i, 1), :] = jnp.max(jnp.abs(piece), axis=0, keepdims=True)
        for part in both:
            held = jnp.zeros((8, 128), F32)
            for j in range(2 * BLOCKS):
                dy = peaks[part, i, 0, j]
                dx = peaks[part, i, 1, j]
                piece = surface[part, j, pl.ds(dy + 6, 8), :]
                shift = lax.rem(8 * j + 2 + 128 - dx, 128)
                held = jnp.where(lane8 == j, pltpu.roll(piece, shift, 1), held)
            windows[part, i] = held

    high = lax.Precision.HIGHEST

    def energy(sums, first):
        return dot(sums[first : first + 5, :] + sums[first + 1 : first + 6, :], spread_ref[...], high) / float(PATCH * PATCH)

    own_energy = [energy(own_sums, 5), energy(own_sums, 0)]

    def finish(part):
        scale = float(PATCH) ** 3 * jnp.sqrt((own_energy[part] + 1e-05) * (energy(other_sums.at[part], 0) + 1e-05))
        lane5 = lax.broadcasted_iota(jnp.int32, (5, 128), 1)
        peak = jnp.zeros((5, 128), F32)
        for j in range(2 * BLOCKS):
            peak = jnp.where(lane5 == j, jnp.max(peak_rows[part, j, 0:5, :], axis=1, keepdims=True), peak)
        height = peak / scale + 1e-05
        rows = jnp.concatenate([jnp.sum(windows[part] * basis_ref[e][None], axis=1) for e in range(6)], 0)
        values = dot(rows, gather_ref[...], high)
        return [values[8 * e : 8 * e + 5] / scale / height for e in range(6)]

    wait_chunk(0)
    other_rows(0)

    def chunk(c, carry):
        wait_chunk(c)
        other_rows(c)
        patch_rows(c - 1)
        return carry

    lax.fori_loop(1, CHUNKS, chunk, 0)
    for e, value in enumerate(finish(BEFORE)):
        result[e, 0:5, :] = value
    pl.when(place.there(copies[ret][0]))(lambda: remote(ret).start())
    for e, value in enumerate(finish(AFTER)):
        out_ref[e, 0:5, 0, :] = value[:, :10]
    for n in range(len(copies)):
        if n != ret:
            pl.when(place.there(copies[n][0]))(lambda: remote(n).wait_send())
    wait_for(ret)
    for e in range(6):
        out_ref[e, 5:10, 0, :] = returned[e, 0:5, :10]
    pl.when(place.there(copies[ret][0]))(lambda: remote(ret).wait_send())


def correlate(tile, peaks):
    tables = host_tables()
    apart = pl.BlockSpec(memory_space=pltpu.HBM)
    count = 5 + 4 * CHUNKS
    return pl.pallas_call(
        kernel,
        out_shape=jax.ShapeDtypeStruct((6, 10, 1, 10), F32),
        in_specs=[apart] * (2 + len(tables)),
        out_specs=pl.BlockSpec(memory_space=pltpu.VMEM),
        scratch_shapes=[
            pltpu.VMEM((ROWS, LANES), BF16),
            pltpu.VMEM((2, PART_ROWS, MAIN), BF16),
            pltpu.VMEM((MAIN // 2, 128), BF16),
            pltpu.VMEM((ROWS // 2, 128), BF16),
            pltpu.VMEM((2, PART_ROWS // 2, 128), BF16),
            *[pltpu.VMEM(t.shape, t.dtype) for t in tables],
            pltpu.VMEM((ROWS, LANES), BF16),
            pltpu.VMEM((ROWS, LANES), BF16),
            pltpu.VMEM((2, PART_ROWS, LANES), BF16),
            pltpu.VMEM((2, PART_ROWS, LANES), BF16),
            pltpu.VMEM((10, 256, LANES), BF16),
            pltpu.VMEM((16, LANES), F32),
            pltpu.VMEM((2, 8, LANES), F32),
            pltpu.VMEM((2, 10, 144, 128), F32),
            pltpu.VMEM((2, 8, 8, 128), F32),
            pltpu.VMEM((2, 10, 8, 128), F32),
            pltpu.VMEM((6, 8, 128), F32),
            pltpu.VMEM((6, 8, 128), F32),
            pltpu.VMEM((5, 2, 10), jnp.int32),
            pltpu.SMEM((2, 5, 2, 10), jnp.int32),
            pltpu.SemaphoreType.DMA((2 + len(tables),)),
            pltpu.SemaphoreType.DMA((count,)),
            pltpu.SemaphoreType.DMA((count,)),
        ],
        compiler_params=pltpu.CompilerParams(
            collective_id=0, has_side_effects=True, vmem_limit_bytes=48 * 1024 * 1024
        ),
    )(tile, peaks, *[jnp.asarray(t) for t in tables])


def body(sections, peaks, valid):
    out = correlate(sections[0], jnp.transpose(peaks, (0, 2, 1, 3))[0])
    return jnp.transpose(out, (2, 0, 1, 3)) * valid[:, None].astype(F32)


def solution(mesh):
    in_specs = (P("gz", "gy", "gx"), P("gz", None, "gy", "gx"), P("gz", "gy", "gx"))
    out_specs = P("gz", None, "gy", "gx")
    return jax.shard_map(body, mesh=mesh, in_specs=in_specs, out_specs=out_specs, check_vma=False)
```

time: 51.4 us -> 38.4 us (0.75)
  the two profiles are of different devices: /device:TPU:203 before, /device:TPU:9 now
where the time goes in v3:
time: 38.4 us; the launch traced here: 38 us
  Pallas kernels  28.3 us (74%)
  local copies, waits for them, and re-layouts  8.32 us (22%)
  other arithmetic  1.33 us (3%)
    pallas_call x1, Pallas kernels, correlate(): pl.pallas_call(kernel, out_shape=jax.ShapeDtypeStruct((6, 10, 1, 10), F32...  28.3 us
    unnamed x20, local copies, waits for them, and re-layouts  8.32 us

profile of v3, /device:TPU:9, one launch (start us, length us, event | category | flops | bytes accessed | tf_op | source)
XLA Modules:
  0.0 38.0 jit_solution(9182293861593519035)
XLA Ops:
  0.0 0.0 copy-start.8
  0.0 0.7 %fusion = f32[10,10]{1,0:T(8,128)S(1)} fusion(s32[1,10,10]{2,0,1:T(1,128)} %param.13), kind=kLoop, calls=%fused_computation.2 | loop fusion | flops 100 | bytes 800 | tf_op jit(solution)/shard_map/convert_element_type | solution.py:402
  0.7 0.1 copy-done.8
  0.8 0.0 copy-start
  0.8 1.1 %copy-done = bf16[1,640,640]{2,1,0:T(8,128)(2,1)S(1)} copy-done((bf16[1,640,640]{2,1,0:T(8,128)(2,1)S(1)}, bf16[1,640,640]{2,1,0:T(8,128)(2,1)}, u32[]{:S(2)}) %copy-start) | copy-done | bytes 819224
  1.9 0.0 copy-start.1
  1.9 1.0 %copy-done.1 = f32[768,128]{1,0:T(8,128)S(1)} copy-done((f32[768,128]{1,0:T(8,128)S(1)}, f32[768,128]{1,0:T(8,128)}, u32[]{:S(2)}) %copy-start.1) | copy-done | bytes 393240
  2.9 0.0 copy-start.2
  2.9 0.9 %copy-done.2 = bf16[2,256,256]{2,1,0:T(8,128)(2,1)S(1)} copy-done((bf16[2,256,256]{2,1,0:T(8,128)(2,1)S(1)}, bf16[2,256,256]{2,1,0:T(8,128)(2,1)}, u32[]{:S(2)}) %copy-start.2) | copy-done | bytes 262168
  3.8 0.0 copy-start.3
  3.8 0.9 %copy-done.3 = bf16[768,128]{1,0:T(8,128)(2,1)S(1)} copy-done((bf16[768,128]{1,0:T(8,128)(2,1)S(1)}, bf16[768,128]{1,0:T(8,128)(2,1)}, u32[]{:S(2)}) %copy-start.3) | copy-done | bytes 196632
  4.8 0.0 copy-start.4
  4.8 0.9 %copy-done.4 = bf16[256,256]{1,0:T(8,128)(2,1)S(1)} copy-done((bf16[256,256]{1,0:T(8,128)(2,1)S(1)}, bf16[256,256]{1,0:T(8,128)(2,1)}, u32[]{:S(2)}) %copy-start.4) | copy-done | bytes 131096
  5.7 0.0 copy-start.5
  5.7 0.9 %copy-done.5 = bf16[256,256]{1,0:T(8,128)(2,1)S(1)} copy-done((bf16[256,256]{1,0:T(8,128)(2,1)S(1)}, bf16[256,256]{1,0:T(8,128)(2,1)}, u32[]{:S(2)}) %copy-start.5) | copy-done | bytes 131096
  6.6 0.0 copy-start.6
  6.6 0.9 %copy-done.6 = bf16[256,256]{1,0:T(8,128)(2,1)S(1)} copy-done((bf16[256,256]{1,0:T(8,128)(2,1)S(1)}, bf16[256,256]{1,0:T(8,128)(2,1)}, u32[]{:S(2)}) %copy-start.6) | copy-done | bytes 131096
  7.5 0.0 copy-start.7
  7.5 0.8 %copy-done.7 = f32[128,128]{1,0:T(8,128)S(1)} copy-done((f32[128,128]{1,0:T(8,128)S(1)}, f32[128,128]{1,0:T(8,128)}, u32[]{:S(2)}) %copy-start.7) | copy-done | bytes 65560
  8.3 0.0 copy-start.9
  8.3 0.7 %copy-done.9 = s32[1,2,10,10]{3,1,2,0:T(2,128)S(1)} copy-done((s32[1,2,10,10]{3,1,2,0:T(2,128)S(1)}, s32[1,2,10,10]{3,1,2,0:T(2,128)}, u32[]{:S(2)}) %copy-start.9) | copy-done | bytes 824
  9.0 28.3 %shard_map.109 = f32[6,10,1,10]{3,2,1,0:T(1,128)S(1)} custom-call(bf16[640,640]{1,0:T(8,128)(2,1)S(1)} %bitcast.8, s32[10,2,10]{2,1,0:T(2,128)S(1)} %bitcast.9, bf16[256,256]{1,0:T(8,128)(2,1)S(1)} %copy-done.6, bf16[768,128]{1,0:T(8,128)(2,1)S(1)} %copy-done.3, bf16[256,256]{1,0:T(8,128)(2,1)S(1)} %copy-done.5, bf16[2,256,256]{2,1,0:T(8,128)(2,1)S(1)} %copy-done.2, ...), custom_call_target="tpu_custom_call" | custom-call | tf_op jit(solution)/shard_map/pallas_call | solution.py:364
  37.3 0.6 %bitcast_multiply_fusion = f32[1,6,10,10]{3,0,2,1:T(1,128)} fusion(f32[6,10,1,10]{3,2,1,0:T(1,128)S(1)} %shard_map.109, f32[10,10]{1,0:T(8,128)S(1)} %fusion), kind=kLoop, calls=%fused_computation | loop fusion | flops 600 | bytes 5200 | tf_op jit(solution)/shard_map/mul | solution.py:402
Async XLA Ops:
  0.0 0.8 %copy-start.8 = (f32[6,8,128]{2,1,0:T(8,128)S(1)}, f32[6,8,128]{2,1,0:T(8,128)}, u32[]{:S(2)}) copy-start(f32[6,8,128]{2,1,0:T(8,128)} %constant.21.clone.basis_hbm) | copy-start | bytes 73732
  0.8 1.1 %copy-start = (bf16[1,640,640]{2,1,0:T(8,128)(2,1)S(1)}, bf16[1,640,640]{2,1,0:T(8,128)(2,1)}, u32[]{:S(2)}) copy-start(bf16[1,640,640]{2,1,0:T(8,128)(2,1)} %param.11) | copy-start | bytes 2457604
  1.9 1.0 %copy-start.1 = (f32[768,128]{1,0:T(8,128)S(1)}, f32[768,128]{1,0:T(8,128)}, u32[]{:S(2)}) copy-start(f32[768,128]{1,0:T(8,128)} %constant.23.clone.spread_hbm) | copy-start | bytes 1179652
  2.9 0.9 %copy-start.2 = (bf16[2,256,256]{2,1,0:T(8,128)(2,1)S(1)}, bf16[2,256,256]{2,1,0:T(8,128)(2,1)}, u32[]{:S(2)}) copy-start(bf16[2,256,256]{2,1,0:T(8,128)(2,1)} %constant.19.clone.inverse_hbm) | copy-start | bytes 786436
  3.8 0.9 %copy-start.3 = (bf16[768,128]{1,0:T(8,128)(2,1)S(1)}, bf16[768,128]{1,0:T(8,128)(2,1)}, u32[]{:S(2)}) copy-start(bf16[768,128]{1,0:T(8,128)(2,1)} %constant.17.clone.nyquist_hbm) | copy-start | bytes 589828
  4.8 0.9 %copy-start.4 = (bf16[256,256]{1,0:T(8,128)(2,1)S(1)}, bf16[256,256]{1,0:T(8,128)(2,1)}, u32[]{:S(2)}) copy-start(bf16[256,256]{1,0:T(8,128)(2,1)} %constant.20.clone.last_hbm) | copy-start | bytes 393220
  5.7 0.9 %copy-start.5 = (bf16[256,256]{1,0:T(8,128)(2,1)S(1)}, bf16[256,256]{1,0:T(8,128)(2,1)}, u32[]{:S(2)}) copy-start(bf16[256,256]{1,0:T(8,128)(2,1)} %constant.18.clone.forward_hbm) | copy-start | bytes 393220
  6.6 0.9 %copy-start.6 = (bf16[256,256]{1,0:T(8,128)(2,1)S(1)}, bf16[256,256]{1,0:T(8,128)(2,1)}, u32[]{:S(2)}) copy-start(bf16[256,256]{1,0:T(8,128)(2,1)} %constant.16.clone.first_hbm) | copy-start | bytes 393220
  7.5 0.8 %copy-start.7 = (f32[128,128]{1,0:T(8,128)S(1)}, f32[128,128]{1,0:T(8,128)}, u32[]{:S(2)}) copy-start(f32[128,128]{1,0:T(8,128)} %constant.22.clone.gather_hbm) | copy-start | bytes 196612
  8.3 0.7 %copy-start.9 = (s32[1,2,10,10]{3,1,2,0:T(2,128)S(1)}, s32[1,2,10,10]{3,1,2,0:T(2,128)}, u32[]{:S(2)}) copy-start(s32[1,2,10,10]{3,1,2,0:T(2,128)} %param.12) | copy-start | bytes 2404

commit v4 on v3

--- a/solution.py
+++ b/solution.py
@@ -392,7 +392,7 @@
             pltpu.SemaphoreType.DMA((count,)),
         ],
         compiler_params=pltpu.CompilerParams(
-            collective_id=0, has_side_effects=True, vmem_limit_bytes=48 * 1024 * 1024
+            collective_id=0, has_side_effects=True, vmem_limit_bytes=62 * 1024 * 1024
         ),
     )(tile, peaks, *[jnp.asarray(t) for t in tables])
 

time: 38.4 us -> 30.2 us (0.79)
  local copies, waits for them, and re-layouts: 8.32 us -> 0 us
  other arithmetic: 1.33 us -> 2.08 us
  Pallas kernels: 28.3 us -> 27.9 us
    unnamed x20 -> x0, local copies, waits for them, and re-layouts: 8.32 us -> none
    mul x1, other arithmetic: 0.63 us -> 1.39 us  [body(): return jnp.transpose(out, (2, 0, 1, 3)) * valid[:, None].astype(F32)]
where the time goes in v4:
time: 30.2 us; the launch traced here: 30 us
  Pallas kernels  27.9 us (92%)
  other arithmetic  2.08 us (7%)
    pallas_call x1, Pallas kernels, correlate(): pl.pallas_call(kernel, out_shape=jax.ShapeDtypeStruct((6, 10, 1, 10), F32...  27.9 us
    mul x1, other arithmetic, body(): return jnp.transpose(out, (2, 0, 1, 3)) * valid[:, None].astype(F32)  1.39 us
    convert_element_type x1, other arithmetic, body(): return jnp.transpose(out, (2, 0, 1, 3)) * valid[:, None].astype(F32)  0.69 us

profile of v4, /device:TPU:9, one launch (start us, length us, event | category | flops | bytes accessed | tf_op | source)
XLA Modules:
  0.0 30.0 jit_solution(553739387369744544)
XLA Ops:
  0.0 0.7 %fusion = f32[10,10]{1,0:T(8,128)S(1)} fusion(s32[1,10,10]{2,0,1:T(1,128)} %param.13), kind=kLoop, calls=%fused_computation.2 | loop fusion | flops 100 | bytes 800 | tf_op jit(solution)/shard_map/convert_element_type | solution.py:402
  0.7 27.9 %shard_map.109 = f32[6,10,1,10]{3,2,1,0:T(1,128)} custom-call(bf16[640,640]{1,0:T(8,128)(2,1)} %bitcast.8, s32[10,2,10]{2,1,0:T(2,128)} %bitcast.9, bf16[256,256]{1,0:T(8,128)(2,1)} %constant.16.clone.first_hbm, bf16[768,128]{1,0:T(8,128)(2,1)} %constant.17.clone.nyquist_hbm, bf16[256,256]{1,0:T(8,128)(2,1)} %constant.18.clone.forward_hbm, ...), custom_call_target="tpu_custom_call" | custom-call | tf_op jit(solution)/shard_map/pallas_call | solution.py:364
  28.6 1.4 %bitcast_multiply_fusion = f32[1,6,10,10]{3,0,2,1:T(1,128)} fusion(f32[6,10,1,10]{3,2,1,0:T(1,128)} %shard_map.109, f32[10,10]{1,0:T(8,128)S(1)} %fusion), kind=kLoop, calls=%fused_computation | loop fusion | flops 600 | bytes 5200 | tf_op jit(solution)/shard_map/mul | solution.py:402

commit v5 on v4

v5 whole, which is shorter than its diff:
```python
import functools
import math

import jax
import jax.numpy as jnp
import ml_dtypes
import numpy as np
from jax import lax
from jax.experimental import pallas as pl
from jax.experimental.pallas import tpu as pltpu
from jax.sharding import PartitionSpec as P

PATCH = 128
STRIDE = 64
WIN = 5
HALF = 64
ROWS = 704
LANES = 768
BLOCKS = 5
STEPS = 5
F32 = jnp.float32
BF16 = jnp.bfloat16


def host_tables():
    index = np.arange(PATCH)
    phase = ((index[:, None] * index[None, :]) % PATCH).astype(np.float32) * np.float32(
        2.0 * math.pi / PATCH
    )
    rounded = lambda v: v.astype(ml_dtypes.bfloat16).astype(np.float32)
    cosine, sine = rounded(np.cos(phase)), rounded(np.sin(phase))
    first = np.zeros((256, 256), np.float32)
    last = np.zeros((256, 256), np.float32)
    weight = np.where(np.arange(HALF) == 0, 1.0, 2.0).astype(np.float32)
    for w in range(2):
        rows = slice(64 * w, 64 * w + 128)
        real, imag = slice(64 * w, 64 * w + 64), slice(128 + 64 * w, 192 + 64 * w)
        lags = slice(128 * w, 128 * w + 128)
        first[rows, real] = cosine[:HALF].T
        first[rows, imag] = -sine[:HALF].T
        first[rows, 128 + 64 * w] = 0.0
        last[real, lags] = (cosine[:, :HALF] * weight).T
        last[imag, lags] = (-sine[:, :HALF] * weight).T
        last[128 + 64 * w, lags] = cosine[:, HALF]
    nyquist = np.zeros((LANES, 128), np.float32)
    for b in range(BLOCKS):
        for w in range(2):
            start = 128 * b + 64 * w
            nyquist[start : start + 128, b + 64 * w] = cosine[HALF]
    forward = np.block([[cosine, sine], [-sine, cosine]])
    inverse = np.stack([np.block([[cosine, sine], [sine, -cosine]]), np.block([[cosine, -sine], [sine, cosine]])])
    offsets = np.arange(WIN, dtype=np.float32) - WIN // 2
    ones = np.ones(WIN, np.float32)
    square = offsets * offsets - np.mean(offsets * offsets)
    pairs = [(ones, ones), (offsets, ones), (ones, offsets), (square, ones), (ones, square), (offsets, offsets)]
    basis = np.zeros((6, 8, 128), np.float32)
    for e, (p, q) in enumerate(pairs):
        func = p[:, None] * q[None, :]
        func = func / np.sqrt(np.sum(func * func))
        for j in range(2 * BLOCKS):
            basis[e, :WIN, 8 * j : 8 * j + WIN] = func
    gather = np.zeros((128, 128), np.float32)
    for j in range(2 * BLOCKS):
        gather[8 * j : 8 * j + 8, j] = 1.0
    spread = np.zeros((LANES, 128), np.float32)
    for j in range(2 * BLOCKS):
        for e in range(6):
            spread[64 * j : 64 * j + 128, 16 * e + j] = 1.0
    low = lambda v: v.astype(ml_dtypes.bfloat16)
    return low(first), low(nyquist), low(forward), low(inverse), low(last), basis, gather, spread


def dot(a, b, precision=None):
    return lax.dot_general(a, b, (((1,), (0,)), ((), ())), precision=precision, preferred_element_type=F32)


def row_transform(x, first_ref, block):
    return dot(x[:, 128 * block : 128 * block + 256], first_ref[...]).astype(BF16)


def unpack(packed):
    wide = packed.astype(F32)
    return jnp.concatenate([wide, pltpu.roll(wide, HALF, 1)], 0).astype(BF16)


def square_sums(x, sums_ref, strip):
    x = x.astype(F32)
    sums_ref[pl.ds(strip, 1), :] = jnp.sum(x * x, axis=0, keepdims=True)


def column_transform(real_ref, imag_ref, start, forward_ref):
    data = jnp.concatenate([real_ref[pl.ds(start, 128), :], imag_ref[pl.ds(start, 128), :]], 0)
    return dot(forward_ref[...], data).astype(BF16)


MAIN = 640


class Place:
    def __init__(self):
        self.at = {name: lax.axis_index(name) for name in ("gz", "gx", "gy")}
        self.size = {name: lax.axis_size(name) for name in ("gz", "gx", "gy")}

    def there(self, step):
        inside = None
        for name, move in zip(("gz", "gx", "gy"), step):
            if not (isinstance(move, int) and move == 0):
                to = self.at[name] + move
                ok = jnp.logical_and(to >= 0, to < self.size[name])
                inside = ok if inside is None else jnp.logical_and(inside, ok)
        return inside

    def device(self, step):
        return {name: self.at[name] + move for name, move in zip(("gz", "gx", "gy"), step)}


def kernel(tile_ref, peaks_ref, valid_hbm, first_hbm, nyquist_hbm, forward_hbm, inverse_hbm, last_hbm, basis_hbm, gather_hbm,
           spread_hbm, out_ref,
           own, other, packed, own_edge, other_edge,
           first_ref, nyquist_ref, forward_ref, inverse_ref, last_ref, basis_ref, gather_ref, spread_ref,
           own_re, own_im, other_re, other_im, spectra, own_sums, other_sums, surface, windows, peak_rows,
           result, returned, far_peaks, valid, peaks, local_sems, send_sems, recv_sems):
    place = Place()
    second = 1 - lax.rem(place.at["gx"], 2)
    is_second = second == 1
    ahead = 2 * second - 1
    tables = [(first_hbm, first_ref), (nyquist_hbm, nyquist_ref), (forward_hbm, forward_ref), (inverse_hbm, inverse_ref),
              (last_hbm, last_ref), (basis_hbm, basis_ref), (gather_hbm, gather_ref), (spread_hbm, spread_ref)]
    main = pl.ds(0, MAIN)
    tile_copy = pltpu.make_async_copy(tile_ref, own.at[main, main], local_sems.at[0])
    local_peaks = pltpu.make_async_copy(peaks_ref, peaks, local_sems.at[1])
    tables.append((valid_hbm, valid))
    local = [pltpu.make_async_copy(a, b, local_sems.at[2 + n]) for n, (a, b) in enumerate(tables)]

    pair = place.there((-ahead, 0, 0))
    beside = place.there((0, 1, 0))
    top = pl.ds(0, STRIDE)
    low = pl.ds(MAIN, STRIDE)
    first32, last32 = pl.ds(0, 32), pl.ds(MAIN // 2, 32)
    copies = [
        ((0, 0, -1), (0, 0, 1), tile_ref.at[top, :], own.at[low, main], None),
        ((0, -1, 0), (0, 1, 0), packed, own_edge.at[pl.ds(0, MAIN // 2)], None),
        ((0, 0, -1), (0, 0, 1), own_edge.at[first32], own_edge.at[last32], beside),
        ((ahead, 0, 0), (-ahead, 0, 0), peaks_ref, far_peaks, is_second),
        ((-ahead, 0, 0), (ahead, 0, 0), result, returned, is_second),
        ((-ahead, -1, 0), (-ahead, 1, 0), packed.at[pl.ds(0, 96)], other_edge.at[pl.ds(0, 96)], None),
        ((-ahead, -1, 0), (-ahead, 1, 0), packed.at[pl.ds(96, 224)], other_edge.at[pl.ds(96, 224)], None),
        ((0, 0, -1), (0, 0, 1), other_edge.at[first32], other_edge.at[last32], jnp.logical_and(pair, beside)),
        ((0, 0, -1), (0, 0, 1), other.at[top, main], other.at[low, main], pair),
    ]
    FAR, RETURN, EDGE, LATER_EDGE, CORNER, FORWARD = 3, 4, 5, 6, 7, 8
    base = len(copies)
    for start, count in [(0, 64)] + [(64 + 128 * t, 128) for t in range(STEPS - 1)] + [(576, 64)]:
        rows = pl.ds(start, count)
        copies.append(((ahead, 0, 0), (-ahead, 0, 0), tile_ref.at[rows, :], other.at[rows, main], None))

    def remote(n):
        step, _, source, destination, _ = copies[n]
        return pltpu.make_async_remote_copy(
            src_ref=source, dst_ref=destination, send_sem=send_sems.at[n], recv_sem=recv_sems.at[n],
            device_id=place.device(step), device_id_type=pl.DeviceIdType.MESH,
        )

    def when(n, side):
        ok = place.there(copies[n][side])
        return ok if copies[n][4] is None else jnp.logical_and(ok, copies[n][4])

    def send(n):
        pl.when(when(n, 0))(lambda: remote(n).start())

    def sent(n):
        pl.when(when(n, 0))(lambda: remote(n).wait_send())

    def wait_for(n):
        pl.when(when(n, 1))(lambda: remote(n).wait_recv())

    @pl.when(place.at["gy"] == place.size["gy"] - 1)
    def _():
        own[MAIN:ROWS, :MAIN] = jnp.zeros((STRIDE, MAIN), BF16)
        own_edge[MAIN // 2 :, :] = jnp.zeros((32, 128), BF16)
        other[MAIN:ROWS, :MAIN] = jnp.zeros((STRIDE, MAIN), BF16)
        other_edge[MAIN // 2 :, :] = jnp.zeros((32, 128), BF16)

    @pl.when(place.at["gx"] == place.size["gx"] - 1)
    def _():
        own_edge[...] = jnp.zeros_like(own_edge)
        other_edge[...] = jnp.zeros_like(other_edge)

    @pl.when(jnp.logical_not(pair))
    def _():
        other[:, :MAIN] = jnp.zeros((ROWS, MAIN), BF16)
        other_edge[...] = jnp.zeros_like(other_edge)
        far_peaks[...] = jnp.zeros_like(far_peaks)

    @pl.when(place.at["gz"] == place.size["gz"] - 1)
    def _():
        returned[...] = jnp.zeros_like(returned)

    barrier = pltpu.get_barrier_semaphore()
    meetings = [((0, 0, -1), (0, 0, 1)), ((0, -1, 0), (0, 1, 0)), ((ahead, 0, 0), (-ahead, 0, 0)),
                ((-ahead, 0, 0), (ahead, 0, 0)), ((-ahead, -1, 0), (-ahead, 1, 0))]
    for _, step in meetings:
        @pl.when(place.there(step))
        def _():
            pl.semaphore_signal(barrier, inc=1, device_id=place.device(step), device_id_type=pl.DeviceIdType.MESH)
    tile_copy.start()
    for copy in local:
        copy.start()
    pl.when(jnp.logical_not(is_second))(lambda: local_peaks.start())
    left = lax.broadcasted_iota(jnp.int32, (32, 128), 1) < HALF
    tile_copy.wait()
    for n in range(MAIN // STRIDE):
        block = own[STRIDE * n : STRIDE * n + STRIDE, 0:128].astype(F32)
        packed[32 * n : 32 * n + 32, :] = jnp.where(left, block[:32], pltpu.roll(block[32:], HALF, 1)).astype(BF16)
    pl.semaphore_wait(barrier, sum(place.there(step).astype(jnp.int32) for step, _ in meetings))
    for n in (1, EDGE, 0, base, FAR, LATER_EDGE, *range(base + 1, len(copies))):
        send(n)

    windows[...] = jnp.zeros_like(windows)
    peak_rows[...] = jnp.zeros_like(peak_rows)
    for copy in local:
        copy.wait()

    def keep(re, im, rows, b, out):
        re[rows, 128 * b : 128 * b + 128] = out[:, :128]
        im[rows, 128 * b : 128 * b + 128] = out[:, 128:]

    def keep_nyquist(re, im, rows, out):
        re[rows, 128 * BLOCKS :] = out
        im[rows, 128 * BLOCKS :] = jnp.zeros((out.shape[0], 128), BF16)

    for b in range(BLOCKS - 1):
        keep(own_re, own_im, slice(0, MAIN), b, row_transform(own[0:MAIN, :], first_ref, b))
    wait_for(1)
    send(2)
    wait_for(base)
    send(FORWARD)
    wait_for(EDGE)
    send(CORNER)
    wait_for(0)
    wait_for(2)

    def own_strip(strip, carry):
        rows = pl.ds(pl.multiple_of(strip * STRIDE, STRIDE), STRIDE)
        own[rows, MAIN:] = unpack(own_edge[pl.ds(pl.multiple_of(strip * 32, 32), 32), :])
        square_sums(own[rows, :], own_sums, strip)
        return carry

    lax.fori_loop(0, ROWS // STRIDE, own_strip, 0)
    for b in range(BLOCKS - 1):
        keep(own_re, own_im, slice(MAIN, ROWS), b, row_transform(own[MAIN:ROWS, :], first_ref, b))
    keep(own_re, own_im, slice(0, ROWS), BLOCKS - 1, row_transform(own[...], first_ref, BLOCKS - 1))
    keep_nyquist(own_re, own_im, slice(0, ROWS), dot(own[...], nyquist_ref[...]).astype(BF16))

    def own_spectra(i, carry):
        for row in (2 * i, 2 * i + 1):
            spectra[row] = column_transform(own_re, own_im, pl.multiple_of(row * STRIDE, STRIDE), forward_ref)
        return carry

    lax.fori_loop(0, 5, own_spectra, 0)
    wait_for(FAR)
    far = pltpu.make_async_copy(far_peaks, peaks, local_sems.at[1])
    pl.when(is_second)(lambda: far.start())
    pl.when(is_second)(lambda: far.wait())
    pl.when(jnp.logical_not(is_second))(lambda: local_peaks.wait())

    lane = lax.broadcasted_iota(jnp.int32, (128, 128), 1)
    slot = lax.rem(lane, HALF) == 0
    lane8 = lax.broadcasted_iota(jnp.int32, (8, 128), 1) // 8

    def other_rows(start, count):
        rows = pl.ds(pl.multiple_of(start, STRIDE), count)
        for k in range(count // STRIDE):
            strip = lax.div(start, STRIDE) + k
            here = pl.ds(pl.multiple_of(strip * STRIDE, STRIDE), STRIDE)
            edge = unpack(other_edge[pl.ds(pl.multiple_of(strip * 32, 32), 32), :])
            other[here, MAIN:] = edge
            square_sums(jnp.concatenate([other[here, :MAIN], edge], 1), other_sums, strip)
        x = other[rows, :]
        for b in range(BLOCKS):
            keep(other_re, other_im, rows, b, row_transform(x, first_ref, b))
        keep_nyquist(other_re, other_im, rows, dot(x, nyquist_ref[...]).astype(BF16))

    def patch_rows(rows):
        crosses = []
        for i in rows:
            a = spectra[i].astype(F32)
            b = column_transform(other_re, other_im, pl.multiple_of(i * STRIDE, STRIDE), forward_ref).astype(F32)
            ar, ai, br, bi = a[:128], a[128:], b[:128], b[128:]
            crosses.append(jnp.concatenate([(ar * br + ai * bi).astype(BF16), (ar * bi - ai * br).astype(BF16)], 0))
        for k, i in enumerate(rows):
            turned = dot(inverse_ref[1 - second], crosses[k])
            extra = turned[:128, 128 * BLOCKS :]
            for b in range(BLOCKS):
                lanes = slice(128 * b, 128 * b + 128)
                moved = extra if b == 0 else pltpu.roll(extra, 128 - b, 1)
                imag = jnp.where(slot, moved, turned[128:, lanes]).astype(BF16)
                out = dot(jnp.concatenate([turned[:128, lanes].astype(BF16), imag], 1), last_ref[...])
                for w in range(2):
                    piece = out[:, 128 * w : 128 * w + 128]
                    j = 2 * b + w
                    surface[k, j, 8:136, :] = piece
                    surface[k, j, 0:8, :] = piece[120:]
                    surface[k, j, 136:144, :] = piece[:8]
                    peak_rows[j, pl.ds(i, 1), :] = jnp.max(jnp.abs(piece), axis=0, keepdims=True)
        for k, i in enumerate(rows):
            held = jnp.zeros((8, 128), F32)
            for j in range(2 * BLOCKS):
                dy = peaks[i, 0, j]
                dx = peaks[i, 1, j]
                piece = surface[k, j, pl.ds(dy + 6, 8), :]
                shift = lax.rem(8 * j + 2 + 128 - dx, 128)
                held = jnp.where(lane8 == j, pltpu.roll(piece, shift, 1), held)
            windows[i] = held

    high = lax.Precision.HIGHEST

    def energy(sums):
        return dot(sums[0:10, :] + sums[1:11, :], spread_ref[...], high) / float(PATCH * PATCH)

    own_energy = energy(own_sums)
    other_rows(jnp.int32(0), STRIDE)

    def step(t, carry):
        start = pl.multiple_of(128 * t + 64, 64)
        rows = other.at[pl.ds(start, 128), main]

        pl.when(t == 1)(lambda: wait_for(LATER_EDGE))

        @pl.when(pair)
        def _():
            pltpu.make_async_remote_copy(
                src_ref=rows, dst_ref=rows, send_sem=send_sems.at[base + 1 + t], recv_sem=recv_sems.at[base + 1 + t],
                device_id=place.device((0, 0, 0)), device_id_type=pl.DeviceIdType.MESH,
            ).wait_recv()

        other_rows(start, 128)
        patch_rows((2 * t, 2 * t + 1))
        return carry

    lax.fori_loop(0, STEPS - 1, step, 0)
    wait_for(base + STEPS)
    wait_for(FORWARD)
    wait_for(CORNER)
    other_rows(jnp.int32(576), 128)
    scale = float(PATCH) ** 3 * jnp.sqrt((own_energy + 1e-05) * (energy(other_sums) + 1e-05))
    patch_rows((8, 9))

    group = lax.rem(lax.broadcasted_iota(jnp.int32, (10, 128), 1), 16)
    peak = jnp.zeros((10, 128), F32)
    for j in range(2 * BLOCKS):
        peak = jnp.where(group == j, jnp.max(peak_rows[j, 0:10, :], axis=1, keepdims=True), peak)
    height = peak / scale + 1e-05
    sums = jnp.concatenate([jnp.sum(windows[...] * basis_ref[e][None], axis=1) for e in range(6)], 0)
    values = dot(sums, gather_ref[...], high)
    joined = values[0:16]
    for e in range(1, 6):
        joined = joined + pltpu.roll(values[16 * e : 16 * e + 16], 16 * e, 1)
    result[0:10, :] = joined[0:10] / scale / height
    send(RETURN)

    def give(coefficients):
        for e in range(6):
            moved = coefficients if e == 0 else pltpu.roll(coefficients, 128 - 16 * e, 1)
            out_ref[e, :, 0, :] = moved[0:10, :10] * valid[:, 0, :].astype(F32)

    for n in range(len(copies)):
        if n != RETURN:
            sent(n)

    @pl.when(jnp.logical_not(is_second))
    def _():
        give(result[...])

    @pl.when(is_second)
    def _():
        wait_for(RETURN)
        give(returned[...])

    sent(RETURN)


def correlate(tile, peaks, valid):
    tables = host_tables()
    apart = pl.BlockSpec(memory_space=pltpu.HBM)
    count = 9 + STEPS + 1
    return pl.pallas_call(
        kernel,
        out_shape=jax.ShapeDtypeStruct((6, 10, 1, 10), F32),
        in_specs=[apart] * (3 + len(tables)),
        out_specs=pl.BlockSpec(memory_space=pltpu.VMEM),
        scratch_shapes=[
            pltpu.VMEM((ROWS, LANES), BF16),
            pltpu.VMEM((ROWS, LANES), BF16),
            pltpu.VMEM((MAIN // 2, 128), BF16),
            pltpu.VMEM((ROWS // 2, 128), BF16),
            pltpu.VMEM((ROWS // 2, 128), BF16),
            *[pltpu.VMEM(t.shape, t.dtype) for t in tables],
            pltpu.VMEM((ROWS, LANES), BF16),
            pltpu.VMEM((ROWS, LANES), BF16),
            pltpu.VMEM((ROWS, LANES), BF16),
            pltpu.VMEM((ROWS, LANES), BF16),
            pltpu.VMEM((10, 256, LANES), BF16),
            pltpu.VMEM((16, LANES), F32),
            pltpu.VMEM((16, LANES), F32),
            pltpu.VMEM((2, 10, 144, 128), F32),
            pltpu.VMEM((16, 8, 128), F32),
            pltpu.VMEM((10, 16, 128), F32),
            pltpu.VMEM((16, 128), F32),
            pltpu.VMEM((16, 128), F32),
            pltpu.VMEM((10, 2, 10), jnp.int32),
            pltpu.VMEM((10, 1, 10), jnp.int32),
            pltpu.SMEM((10, 2, 10), jnp.int32),
            pltpu.SemaphoreType.DMA((3 + len(tables),)),
            pltpu.SemaphoreType.DMA((count,)),
            pltpu.SemaphoreType.DMA((count,)),
        ],
        compiler_params=pltpu.CompilerParams(
            collective_id=0, has_side_effects=True, vmem_limit_bytes=62 * 1024 * 1024
        ),
    )(tile, peaks, valid, *[jnp.asarray(t) for t in tables])


def body(sections, peaks, valid):
    out = correlate(sections[0], jnp.transpose(peaks, (0, 2, 1, 3))[0], jnp.transpose(valid, (1, 0, 2)))
    return jnp.transpose(out, (2, 0, 1, 3))


def solution(mesh):
    in_specs = (P("gz", "gy", "gx"), P("gz", None, "gy", "gx"), P("gz", "gy", "gx"))
    out_specs = P("gz", None, "gy", "gx")
    return jax.shard_map(body, mesh=mesh, in_specs=in_specs, out_specs=out_specs, check_vma=False)
```

time: 30.2 us -> 28.7 us (0.950)
  other arithmetic: 2.08 us -> 0 us
  local copies, waits for them, and re-layouts: 0 us -> 1.37 us
  Pallas kernels: 27.9 us -> 27.1 us
    mul x1 -> x0, other arithmetic: 1.39 us -> none  [body(): return jnp.transpose(out, (2, 0, 1, 3)) * valid[:, None].astype(F32)]
    unnamed x0 -> x1, local copies, waits for them, and re-layouts: none -> 1.37 us
    pallas_call x1, Pallas kernels: 27.9 us -> 27.1 us  [correlate(): pl.pallas_call(kernel, out_shape=jax.ShapeDtypeStruct((6, 10, 1, 10), F32...]
    convert_element_type x1 -> x0, other arithmetic: 0.69 us -> none  [body(): return jnp.transpose(out, (2, 0, 1, 3)) * valid[:, None].astype(F32)]
where the time goes in v5:
time: 28.7 us; the launch traced here: 28.5 us
  Pallas kernels  27.1 us (94%)
  local copies, waits for them, and re-layouts  1.37 us (5%)
    pallas_call x1, Pallas kernels, correlate(): pl.pallas_call(kernel, out_shape=jax.ShapeDtypeStruct((6, 10, 1, 10), F32...  27.1 us
    unnamed x1, local copies, waits for them, and re-layouts  1.37 us

profile of v5, /device:TPU:9, one launch (start us, length us, event | category | flops | bytes accessed | tf_op | source)
XLA Modules:
  0.0 28.5 jit_solution(5952936588308702936)
XLA Ops:
  0.0 27.1 %shard_map.109 = f32[6,10,1,10]{3,2,1,0:T(1,128)} custom-call(bf16[640,640]{1,0:T(8,128)(2,1)} %bitcast.6, s32[10,2,10]{2,1,0:T(2,128)} %bitcast.8, s32[10,1,10]{2,1,0:T(1,128)} %bitcast.9, bf16[256,256]{1,0:T(8,128)(2,1)} %constant.16.clone.first_hbm, bf16[768,128]{1,0:T(8,128)(2,1)} %constant.17.clone.nyquist_hbm, ...), custom_call_target="tpu_custom_call" | custom-call | tf_op jit(solution)/shard_map/pallas_call | solution.py:387
  27.1 1.4 %copy.13 = f32[1,6,10,10]{3,0,2,1:T(1,128)} copy(f32[1,6,10,10]{3,0,2,1:T(1,128)} %bitcast.7) | data formatting | bytes 4800

commit v6 on v5

--- a/solution.py
+++ b/solution.py
@@ -88,8 +88,8 @@
     sums_ref[pl.ds(strip, 1), :] = jnp.sum(x * x, axis=0, keepdims=True)
 
 
-def column_transform(real_ref, imag_ref, start, forward_ref):
-    data = jnp.concatenate([real_ref[pl.ds(start, 128), :], imag_ref[pl.ds(start, 128), :]], 0)
+def column_transform(real_ref, imag_ref, start, forward_ref, lanes=slice(0, LANES)):
+    data = jnp.concatenate([real_ref[pl.ds(start, 128), lanes], imag_ref[pl.ds(start, 128), lanes]], 0)
     return dot(forward_ref[...], data).astype(BF16)
 
 
@@ -231,13 +231,37 @@
 
     for b in range(BLOCKS - 1):
         keep(own_re, own_im, slice(0, MAIN), b, row_transform(own[0:MAIN, :], first_ref, b))
-    wait_for(1)
-    send(2)
+    near, distant = is_second, jnp.logical_not(is_second)
+
+    def pass_own_corner():
+        wait_for(1)
+        send(2)
+
+    def pass_corner():
+        wait_for(EDGE)
+        send(CORNER)
+
+    pl.when(near)(pass_own_corner)
     wait_for(base)
     send(FORWARD)
-    wait_for(EDGE)
-    send(CORNER)
+    pl.when(near)(pass_corner)
     wait_for(0)
+    for b in range(BLOCKS - 1):
+        keep(own_re, own_im, slice(MAIN, ROWS), b, row_transform(own[MAIN:ROWS, :], first_ref, b))
+
+    def own_spectra(lanes, count):
+        def some(i, carry):
+            for k in range(count):
+                row = count * i + k
+                start = pl.multiple_of(row * STRIDE, STRIDE)
+                spectra[row, :, lanes] = column_transform(own_re, own_im, start, forward_ref, lanes)
+            return carry
+
+        lax.fori_loop(0, 10 // count, some, 0)
+
+    pl.when(distant)(lambda: own_spectra(slice(0, 512), 5))
+    pl.when(distant)(pass_own_corner)
+    pl.when(distant)(pass_corner)
     wait_for(2)
 
     def own_strip(strip, carry):
@@ -247,20 +271,13 @@
         return carry
 
     lax.fori_loop(0, ROWS // STRIDE, own_strip, 0)
-    for b in range(BLOCKS - 1):
-        keep(own_re, own_im, slice(MAIN, ROWS), b, row_transform(own[MAIN:ROWS, :], first_ref, b))
     keep(own_re, own_im, slice(0, ROWS), BLOCKS - 1, row_transform(own[...], first_ref, BLOCKS - 1))
     keep_nyquist(own_re, own_im, slice(0, ROWS), dot(own[...], nyquist_ref[...]).astype(BF16))
-
-    def own_spectra(i, carry):
-        for row in (2 * i, 2 * i + 1):
-            spectra[row] = column_transform(own_re, own_im, pl.multiple_of(row * STRIDE, STRIDE), forward_ref)
-        return carry
-
-    lax.fori_loop(0, 5, own_spectra, 0)
     wait_for(FAR)
     far = pltpu.make_async_copy(far_peaks, peaks, local_sems.at[1])
     pl.when(is_second)(lambda: far.start())
+    pl.when(near)(lambda: own_spectra(slice(0, LANES), 2))
+    pl.when(distant)(lambda: own_spectra(slice(512, LANES), 10))
     pl.when(is_second)(lambda: far.wait())
     pl.when(jnp.logical_not(is_second))(lambda: local_peaks.wait())
 
@@ -284,10 +301,10 @@
     def patch_rows(rows):
         crosses = []
         for i in rows:
-            a = spectra[i].astype(F32)
-            b = column_transform(other_re, other_im, pl.multiple_of(i * STRIDE, STRIDE), forward_ref).astype(F32)
+            a = spectra[i]
+            b = column_transform(other_re, other_im, pl.multiple_of(i * STRIDE, STRIDE), forward_ref)
             ar, ai, br, bi = a[:128], a[128:], b[:128], b[128:]
-            crosses.append(jnp.concatenate([(ar * br + ai * bi).astype(BF16), (ar * bi - ai * br).astype(BF16)], 0))
+            crosses.append(jnp.concatenate([ar * br + ai * bi, ar * bi - ai * br], 0))
         for k, i in enumerate(rows):
             turned = dot(inverse_ref[1 - second], crosses[k])
             extra = turned[:128, 128 * BLOCKS :]

time: 28.7 us -> 27 us (0.941)
  the two profiles are of different devices: /device:TPU:9 before, /device:TPU:30 now
where the time goes in v6:
time: 27 us; the launch traced here: 26.9 us
  Pallas kernels  25.5 us (94%)
  local copies, waits for them, and re-layouts  1.37 us (5%)
    pallas_call x1, Pallas kernels, correlate(): pl.pallas_call(kernel, out_shape=jax.ShapeDtypeStruct((6, 10, 1, 10), F32...  25.5 us
    unnamed x1, local copies, waits for them, and re-layouts  1.37 us

profile of v6, /device:TPU:30, one launch (start us, length us, event | category | flops | bytes accessed | tf_op | source)
XLA Modules:
  0.0 26.9 jit_solution(15106438763072219931)
XLA Ops:
  0.0 25.5 %shard_map.109 = f32[6,10,1,10]{3,2,1,0:T(1,128)} custom-call(bf16[640,640]{1,0:T(8,128)(2,1)} %bitcast.6, s32[10,2,10]{2,1,0:T(2,128)} %bitcast.8, s32[10,1,10]{2,1,0:T(1,128)} %bitcast.9, bf16[256,256]{1,0:T(8,128)(2,1)} %constant.16.clone.first_hbm, bf16[768,128]{1,0:T(8,128)(2,1)} %constant.17.clone.nyquist_hbm, ...), custom_call_target="tpu_custom_call" | custom-call | tf_op jit(solution)/shard_map/pallas_call | solution.py:404
  25.5 1.4 %copy.13 = f32[1,6,10,10]{3,0,2,1:T(1,128)} copy(f32[1,6,10,10]{3,0,2,1:T(1,128)} %bitcast.7) | data formatting | bytes 4800

commit v7 on v6

--- a/solution.py
+++ b/solution.py
@@ -67,11 +67,21 @@
         for e in range(6):
             spread[64 * j : 64 * j + 128, 16 * e + j] = 1.0
     low = lambda v: v.astype(ml_dtypes.bfloat16)
-    return low(first), low(nyquist), low(forward), low(inverse), low(last), basis, gather, spread
+    return low(first), low(nyquist), low(forward), low(inverse), low(last), basis, low(gather), low(spread)
 
 
 def dot(a, b, precision=None):
     return lax.dot_general(a, b, (((1,), (0,)), ((), ())), precision=precision, preferred_element_type=F32)
+
+
+def exact_dot(x, table):
+    high = x.astype(BF16)
+    rest = x - high.astype(F32)
+    middle = rest.astype(BF16)
+    low = (rest - middle.astype(F32)).astype(BF16)
+    count = x.shape[0]
+    out = dot(jnp.concatenate([high, middle, low], 0), table)
+    return out[:count] + out[count : 2 * count] + out[2 * count :]
 
 
 def row_transform(x, first_ref, block):
@@ -259,7 +269,7 @@
 
         lax.fori_loop(0, 10 // count, some, 0)
 
-    pl.when(distant)(lambda: own_spectra(slice(0, 512), 5))
+    pl.when(distant)(lambda: own_spectra(slice(0, 512), 10))
     pl.when(distant)(pass_own_corner)
     pl.when(distant)(pass_corner)
     wait_for(2)
@@ -270,13 +280,13 @@
         square_sums(own[rows, :], own_sums, strip)
         return carry
 
-    lax.fori_loop(0, ROWS // STRIDE, own_strip, 0)
+    lax.fori_loop(0, ROWS // STRIDE, own_strip, 0, unroll=True)
     keep(own_re, own_im, slice(0, ROWS), BLOCKS - 1, row_transform(own[...], first_ref, BLOCKS - 1))
     keep_nyquist(own_re, own_im, slice(0, ROWS), dot(own[...], nyquist_ref[...]).astype(BF16))
     wait_for(FAR)
     far = pltpu.make_async_copy(far_peaks, peaks, local_sems.at[1])
     pl.when(is_second)(lambda: far.start())
-    pl.when(near)(lambda: own_spectra(slice(0, LANES), 2))
+    pl.when(near)(lambda: own_spectra(slice(0, LANES), 10))
     pl.when(distant)(lambda: own_spectra(slice(512, LANES), 10))
     pl.when(is_second)(lambda: far.wait())
     pl.when(jnp.logical_not(is_second))(lambda: local_peaks.wait())
@@ -330,10 +340,9 @@
                 held = jnp.where(lane8 == j, pltpu.roll(piece, shift, 1), held)
             windows[i] = held
 
-    high = lax.Precision.HIGHEST
-
     def energy(sums):
-        return dot(sums[0:10, :] + sums[1:11, :], spread_ref[...], high) / float(PATCH * PATCH)
+        rows = jnp.concatenate([sums[0:10, :] + sums[1:11, :], jnp.zeros((6, LANES), F32)], 0)
+        return exact_dot(rows, spread_ref[...])[0:10] / float(PATCH * PATCH)
 
     own_energy = energy(own_sums)
     other_rows(jnp.int32(0), STRIDE)
@@ -369,7 +378,7 @@
         peak = jnp.where(group == j, jnp.max(peak_rows[j, 0:10, :], axis=1, keepdims=True), peak)
     height = peak / scale + 1e-05
     sums = jnp.concatenate([jnp.sum(windows[...] * basis_ref[e][None], axis=1) for e in range(6)], 0)
-    values = dot(sums, gather_ref[...], high)
+    values = exact_dot(sums, gather_ref[...])
     joined = values[0:16]
     for e in range(1, 6):
         joined = joined + pltpu.roll(values[16 * e : 16 * e + 16], 16 * e, 1)

time: 27 us -> 25.4 us (0.941)
  the two profiles are of different devices: /device:TPU:30 before, /device:TPU:9 now
where the time goes in v7:
time: 25.4 us; the launch traced here: 25.2 us
  Pallas kernels  23.9 us (94%)
  local copies, waits for them, and re-layouts  1.37 us (5%)
    pallas_call x1, Pallas kernels, correlate(): pl.pallas_call(kernel, out_shape=jax.ShapeDtypeStruct((6, 10, 1, 10), F32...  23.9 us
    unnamed x1, local copies, waits for them, and re-layouts  1.37 us

profile of v7, /device:TPU:9, one launch (start us, length us, event | category | flops | bytes accessed | tf_op | source)
XLA Modules:
  0.0 25.2 jit_solution(8153452150913633216)
XLA Ops:
  0.0 23.9 %shard_map.109 = f32[6,10,1,10]{3,2,1,0:T(1,128)} custom-call(bf16[640,640]{1,0:T(8,128)(2,1)} %bitcast.6, s32[10,2,10]{2,1,0:T(2,128)} %bitcast.8, s32[10,1,10]{2,1,0:T(1,128)} %bitcast.9, bf16[256,256]{1,0:T(8,128)(2,1)} %constant.16.clone.first_hbm, bf16[768,128]{1,0:T(8,128)(2,1)} %constant.17.clone.nyquist_hbm, ...), custom_call_target="tpu_custom_call" | custom-call | tf_op jit(solution)/shard_map/pallas_call | solution.py:413
  23.9 1.4 %copy.13 = f32[1,6,10,10]{3,0,2,1:T(1,128)} copy(f32[1,6,10,10]{3,0,2,1:T(1,128)} %bitcast.7) | data formatting | bytes 4800

commit v8 on v7

--- a/solution.py
+++ b/solution.py
@@ -310,13 +310,14 @@
 
     def patch_rows(rows):
         crosses = []
-        for i in rows:
+        theirs = [column_transform(other_re, other_im, pl.multiple_of(i * STRIDE, STRIDE), forward_ref) for i in rows]
+        for i, b in zip(rows, theirs):
             a = spectra[i]
-            b = column_transform(other_re, other_im, pl.multiple_of(i * STRIDE, STRIDE), forward_ref)
             ar, ai, br, bi = a[:128], a[128:], b[:128], b[128:]
             crosses.append(jnp.concatenate([ar * br + ai * bi, ar * bi - ai * br], 0))
+        turns = [dot(inverse_ref[1 - second], cross) for cross in crosses]
         for k, i in enumerate(rows):
-            turned = dot(inverse_ref[1 - second], crosses[k])
+            turned = turns[k]
             extra = turned[:128, 128 * BLOCKS :]
             for b in range(BLOCKS):
                 lanes = slice(128 * b, 128 * b + 128)

time: 25.4 us -> 24.8 us (0.976)
  the two profiles are of different devices: /device:TPU:9 before, /device:TPU:30 now
where the time goes in v8:
time: 24.8 us; the launch traced here: 24.7 us
  Pallas kernels  23.3 us (94%)
  local copies, waits for them, and re-layouts  1.37 us (6%)
    pallas_call x1, Pallas kernels, correlate(): pl.pallas_call(kernel, out_shape=jax.ShapeDtypeStruct((6, 10, 1, 10), F32...  23.3 us
    unnamed x1, local copies, waits for them, and re-layouts  1.37 us

profile of v8, /device:TPU:30, one launch (start us, length us, event | category | flops | bytes accessed | tf_op | source)
XLA Modules:
  0.0 24.7 jit_solution(15104415722364603360)
XLA Ops:
  0.0 23.3 %shard_map.109 = f32[6,10,1,10]{3,2,1,0:T(1,128)} custom-call(bf16[640,640]{1,0:T(8,128)(2,1)} %bitcast.6, s32[10,2,10]{2,1,0:T(2,128)} %bitcast.8, s32[10,1,10]{2,1,0:T(1,128)} %bitcast.9, bf16[256,256]{1,0:T(8,128)(2,1)} %constant.16.clone.first_hbm, bf16[768,128]{1,0:T(8,128)(2,1)} %constant.17.clone.nyquist_hbm, ...), custom_call_target="tpu_custom_call" | custom-call | tf_op jit(solution)/shard_map/pallas_call | solution.py:414
  23.3 1.4 %copy.13 = f32[1,6,10,10]{3,0,2,1:T(1,128)} copy(f32[1,6,10,10]{3,0,2,1:T(1,128)} %bitcast.7) | data formatting | bytes 4800

commit v9 on v8

--- a/solution.py
+++ b/solution.py
@@ -365,7 +365,8 @@
         patch_rows((2 * t, 2 * t + 1))
         return carry
 
-    lax.fori_loop(0, STEPS - 1, step, 0)
+    for t in range(STEPS - 1):
+        step(jnp.int32(t), 0)
     wait_for(base + STEPS)
     wait_for(FORWARD)
     wait_for(CORNER)

time: 24.8 us -> 24.7 us (level)
  no operation moved by 1% of the time
where the time goes in v9:
time: 24.7 us; the launch traced here: 24.5 us
  Pallas kernels  23.1 us (94%)
  local copies, waits for them, and re-layouts  1.37 us (6%)
    pallas_call x1, Pallas kernels, correlate(): pl.pallas_call(kernel, out_shape=jax.ShapeDtypeStruct((6, 10, 1, 10), F32...  23.1 us
    unnamed x1, local copies, waits for them, and re-layouts  1.37 us

profile of v9, /device:TPU:30, one launch (start us, length us, event | category | flops | bytes accessed | tf_op | source)
XLA Modules:
  0.0 24.5 jit_solution(2578349938698910586)
XLA Ops:
  0.0 23.1 %shard_map.109 = f32[6,10,1,10]{3,2,1,0:T(1,128)} custom-call(bf16[640,640]{1,0:T(8,128)(2,1)} %bitcast.6, s32[10,2,10]{2,1,0:T(2,128)} %bitcast.8, s32[10,1,10]{2,1,0:T(1,128)} %bitcast.9, bf16[256,256]{1,0:T(8,128)(2,1)} %constant.16.clone.first_hbm, bf16[768,128]{1,0:T(8,128)(2,1)} %constant.17.clone.nyquist_hbm, ...), custom_call_target="tpu_custom_call" | custom-call | tf_op jit(solution)/shard_map/pallas_call | solution.py:415
  23.1 1.4 %copy.13 = f32[1,6,10,10]{3,0,2,1:T(1,128)} copy(f32[1,6,10,10]{3,0,2,1:T(1,128)} %bitcast.7) | data formatting | bytes 4800
